TPU v7x, 128 devices: a whole 4x4x4 slice. The times are simulated.
128 devices in a mesh: leaf: 16 (over y, z), pts: 8 (over x, core).
Axes of the slice: x: 4, y: 4, z: 4, core: 2. Of those that a mesh axis runs over, the one named last changes fastest.
Arguments:
- vectors: float32 [32, 524288], P(None, ('leaf', 'pts')), may hold values from -6 to 6
- points: float32 [3, 524288], P(None, ('leaf', 'pts')), may hold values from 0 to 1
- leaf_bases: float32 [2048, 64, 256], P(('leaf', 'pts')), may hold values from -0.375 to 0.375
- local_transfer: float32 [128, 30, 64, 64], P(('leaf', 'pts')), may hold values from -0.5 to 0.5
- skel_points: float32 [3, 229376], P(None, ('leaf', 'pts')), may hold values from 0 to 1
- up_transfer: float32 [254, 64, 64], replicated, may hold values from -0.5 to 0.5
- up_points: float32 [3, 16256], replicated, may hold values from 0 to 1
- source_ids: int32 [3, 128, 128, 2], P(None, ('leaf', 'pts')), may hold values from 0 to 2047, as said below
- target_ids: int32 [3, 128, 128, 2], P(None, ('leaf', 'pts')), may hold values from 0 to 2047, as said below
- live_counts: int32 [3, 128, 128], P(None, ('leaf', 'pts')), may hold values from 0 to 2, as said below
Outputs:
- product: float32 [32, 524288], P(None, ('leaf', 'pts'))
Inputs may be any that keep to these rules, and one draw needn't show every extreme that they name: source_ids[l, s, d, k] is a node of level l owned by device s: s * (16 / 2**l) + j with j below 16 / 2**l; slots at or past the count hold such ids too. target_ids[l, d, s, k] is a node of level l owned by device d, in the same way. `live_counts`: at each level some device has all 2 slots used from every sending device.
All inputs are finite; a program needn't handle non-finite values.
Results may differ from a plain program's by a relative error of at most 0.0003.
Values sent between devices are 32-bit elements; how exact they have to be, the bound alone decides.
A program may use at most 192 MiB of HBM per device.

v0:
```python
import math

import jax
import jax.numpy as jnp
from jax import lax
from jax.sharding import PartitionSpec as P

PRECISE = lax.Precision.HIGHEST
SCALE_FACTOR = math.sqrt(3.0) / 0.3


def extended(value, sides, width):
    for axis, dim in sides:
        size, length = (lax.axis_size(axis), value.shape[dim])
        up = [(i, (i + 1) % size) for i in range(size - 1)]
        down = [(j, i) for i, j in up]
        last = lax.slice_in_dim(value, length - width, length, axis=dim)
        first = lax.slice_in_dim(value, 0, width, axis=dim)
        before = lax.ppermute(last, axis, up)
        after = lax.ppermute(first, axis, down)
        value = jnp.concatenate([before, value, after], axis=dim)
    return value


def swapped(block, axis, distance):
    count = lax.axis_size(axis)
    route = []
    for low in range(count):
        high = low | 1 << distance
        if high != low and high < count:
            route += [(low, high), (high, low)]
    return lax.ppermute(block, axis, route)


def matern(left_pts, right_pts):
    squared = (left_pts[..., 0, :, None] - right_pts[..., 0, None, :]) ** 2
    squared = squared + (left_pts[..., 1, :, None] - right_pts[..., 1, None, :]) ** 2
    squared = squared + (left_pts[..., 2, :, None] - right_pts[..., 2, None, :]) ** 2
    scaled = jnp.sqrt(squared) * SCALE_FACTOR
    return (1.0 + scaled) * jnp.exp(-scaled)


def matern_blocks(left_pts, right_pts):
    squared = (left_pts[0][:, :, None] - right_pts[0][:, None, :]) ** 2
    squared = squared + (left_pts[1][:, :, None] - right_pts[1][:, None, :]) ** 2
    squared = squared + (left_pts[2][:, :, None] - right_pts[2][:, None, :]) ** 2
    scaled = jnp.sqrt(squared) * SCALE_FACTOR
    return (1.0 + scaled) * jnp.exp(-scaled)


def level_offset(height, count):
    if height == 0:
        return 0
    return 2 * count - (count >> height - 1)


def climb(upward, sibling, height, own_index, up_transfer, up_points, device_count):
    rank_size = up_transfer.shape[1]
    offset = level_offset(height, device_count)
    node_id = jnp.right_shift(own_index, height)
    first_child = node_id - node_id % 2
    is_left = node_id % 2 == 0
    left_part = jnp.where(is_left, upward, sibling)
    right_part = jnp.where(is_left, sibling, upward)
    left_matrix = lax.dynamic_index_in_dim(up_transfer, offset + first_child, 0, keepdims=False)
    right_matrix = lax.dynamic_index_in_dim(
        up_transfer, offset + first_child + 1, 0, keepdims=False
    )
    parent = jnp.dot(left_part, left_matrix.T, precision=PRECISE) + jnp.dot(
        right_part, right_matrix.T, precision=PRECISE
    )
    own_points = lax.dynamic_slice_in_dim(up_points, (offset + node_id) * rank_size, rank_size, 1)
    other_points = lax.dynamic_slice_in_dim(
        up_points, (offset + jnp.bitwise_xor(node_id, 1)) * rank_size, rank_size, 1
    )
    coupled = jnp.dot(sibling, matern(own_points, other_points).T, precision=PRECISE)
    own_matrix = lax.dynamic_index_in_dim(up_transfer, offset + node_id, 0, keepdims=False)
    return (parent, coupled, own_matrix)


def route_blocks(send_coefs, send_points):
    got_coefs, got_points = (
        lax.all_to_all(send_coefs, ("leaf", "pts"), split_axis=0, concat_axis=0, tiled=True),
        lax.all_to_all(send_points, ("leaf", "pts"), split_axis=0, concat_axis=0, tiled=True),
    )
    return (got_coefs, got_points)


def on_device(
    vectors,
    points,
    leaf_bases,
    local_transfer,
    skel_points,
    up_transfer,
    up_points,
    source_ids,
    target_ids,
    live_counts,
):
    leaf_count = leaf_bases.shape[0]
    rank_size = leaf_bases.shape[1]
    leaf_size = leaf_bases.shape[2]
    vec_count = vectors.shape[0]
    list_levels = source_ids.shape[0]
    slot_count = source_ids.shape[3]
    device_count = lax.axis_size(("leaf", "pts"))
    own_index = lax.axis_index(("leaf", "pts"))
    stacked = jnp.concatenate([vectors, points], axis=0)
    widened = extended(stacked, ((("leaf", "pts"), 1),), leaf_size)
    blocks = widened.reshape(vec_count + 3, leaf_count + 2, leaf_size)
    own_points = points.reshape(3, leaf_count, leaf_size)
    near_field = jnp.zeros((vec_count, leaf_count, leaf_size), jnp.float32)
    for neighbour in range(3):
        near_block = blocks[:, neighbour : neighbour + leaf_count]
        kernel = matern_blocks(own_points, near_block[vec_count:])
        near_field = near_field + jnp.einsum(
            "mpq,vmq->vmp", kernel, near_block[:vec_count], precision=PRECISE
        )
    leaf_vectors = vectors.reshape(vec_count, leaf_count, leaf_size)
    coefficients = [jnp.einsum("mip,vmp->mvi", leaf_bases, leaf_vectors, precision=PRECISE)]
    top_local = leaf_count.bit_length() - 1
    matrices = []
    for height in range(top_local):
        node_count = leaf_count >> height
        offset = level_offset(height, leaf_count)
        matrix = local_transfer[0, offset : offset + node_count]
        moved_up = jnp.einsum("nij,nvj->nvi", matrix, coefficients[-1], precision=PRECISE)
        paired = moved_up.reshape(node_count // 2, 2, vec_count, rank_size)
        coefficients.append(paired[:, 0] + paired[:, 1])
        matrices.append(matrix)
    upper_levels = device_count.bit_length() - 1
    upward = coefficients[-1][0]
    couples = []
    own_mats = []
    height = 0
    for bit_index in range(lax.axis_size("pts").bit_length() - 1):
        sibling = swapped(upward, "pts", bit_index)
        upward, coupled, own_matrix = climb(
            upward, sibling, height, own_index, up_transfer, up_points, device_count
        )
        couples.append(coupled)
        own_mats.append(own_matrix)
        height += 1
    for bit_index in range(lax.axis_size("leaf").bit_length() - 1):
        sibling = swapped(upward, "leaf", bit_index)
        upward, coupled, own_matrix = climb(
            upward, sibling, height, own_index, up_transfer, up_points, device_count
        )
        couples.append(coupled)
        own_mats.append(own_matrix)
        height += 1
    far_top = couples[-1]
    for height in range(upper_levels - 2, -1, -1):
        far_top = couples[height] + jnp.dot(far_top, own_mats[height], precision=PRECISE)
    level_pointsets = []
    send_coef_list = []
    send_point_list = []
    for height in range(list_levels):
        node_count = leaf_count >> height
        offset = level_offset(height, leaf_count)
        level_points = skel_points[
            :, offset * rank_size : (offset + node_count) * rank_size
        ].reshape(3, node_count, rank_size)
        level_pointsets.append(level_points)
        sources = source_ids[height, 0] - own_index * node_count
        send_coef_list.append(coefficients[height][sources])
        send_point_list.append(jnp.moveaxis(level_points[:, sources], 0, 2))
    received = []
    for height in range(list_levels):
        received.append(route_blocks(send_coef_list[height], send_point_list[height]))
    couplings = []
    for height in range(list_levels):
        node_count = leaf_count >> height
        got_coefs, got_points = received[height]
        targets = target_ids[height, 0] - own_index * node_count
        target_points = jnp.moveaxis(level_pointsets[height][:, targets], 0, 2)
        kernel_list = matern(target_points, got_points)
        products = jnp.einsum("scij,scvj->scvi", kernel_list, got_coefs, precision=PRECISE)
        live_mask = (
            jnp.arange(slot_count, dtype=jnp.int32)[None, :] < live_counts[height, 0][:, None]
        )
        onehot = (
            (targets.reshape(-1)[None, :] == jnp.arange(node_count, dtype=jnp.int32)[:, None])
            & live_mask.reshape(-1)[None, :]
        ).astype(jnp.float32)
        summed = jnp.dot(
            onehot,
            products.reshape(device_count * slot_count, vec_count * rank_size),
            precision=PRECISE,
        )
        couplings.append(summed.reshape(node_count, vec_count, rank_size))
    downward = far_top[None]
    for height in range(top_local - 1, -1, -1):
        downward = jnp.einsum(
            "nvi,nij->nvj", jnp.repeat(downward, 2, axis=0), matrices[height], precision=PRECISE
        )
        if height < list_levels:
            downward = downward + couplings[height]
    far_field = jnp.einsum("mip,mvi->vmp", leaf_bases, downward, precision=PRECISE)
    return (near_field + far_field).reshape(vec_count, leaf_count * leaf_size)


def solution(mesh):
    return jax.shard_map(
        on_device,
        mesh=mesh,
        in_specs=(
            P(None, ("leaf", "pts")),
            P(None, ("leaf", "pts")),
            P(("leaf", "pts"), None, None),
            P(("leaf", "pts"), None, None, None),
            P(None, ("leaf", "pts")),
            P(),
            P(),
            P(None, ("leaf", "pts"), None, None),
            P(None, ("leaf", "pts"), None, None),
            P(None, ("leaf", "pts"), None),
        ),
        out_specs=P(None, ("leaf", "pts")),
        check_vma=False,
    )
```

profile of v0, /device:TPU:1, one launch (start us, length us, event | category | flops | bytes accessed | tf_op | source)
XLA Modules:
  0.0 449.6 jit_solution(7382623723411482794)
XLA Ops:
  15.3 10.2 %all-to-all-start.1 = ((f32[128,1,384]{2,1,0:T(1,128)}), f32[128,1,384]{2,1,0:T(1,128)S(1)}, u32[]{:S(2)}, u32[]{:S(2)}) async-start(f32[128,1,384]{2,1,0:T(1,128)} %reshape.431), calls=%async_computation.1 | async-start | bytes 393216 | tf_op jit(solution)/shard_map/all_to_all | solution.py:84
  55.6 30.6 %constant_dynamic-slice_fusion = (f32[1,64,64]{0,2,1:T(8,128)}, f32[1,64,64]{0,2,1:T(8,128)}, f32[1,64,64]{0,2,1:T(8,128)}, f32[1,64,64]{0,2,1:T(8,128)}, f32[1,...) fusion(f32[254,64,64]{0,2,1:T(8,128)} %param.15, ...), kind=kLoop, calls=%fused_computation.436 | loop fusion | bytes 589896 | tf_op jit(solution)/shard_map/jit(dynamic_index_in_dim)/dynamic_slice | solution.py:77
  158.8 5.5 %reshape.429 = f32[128,1,4096]{2,1,0:T(1,128)} reshape(f32[128,2,32,64]{3,2,1,0:T(8,128)} %bitcast.368) | data formatting | bytes 4194304
  167.7 5.5 %reshape.433 = f32[128,1,4096]{2,1,0:T(1,128)} reshape(f32[128,2,32,64]{3,2,1,0:T(8,128)} %bitcast.367) | data formatting | bytes 4194304
  177.2 5.5 %reshape.437 = f32[128,1,4096]{2,1,0:T(1,128)} reshape(f32[128,2,32,64]{3,2,1,0:T(8,128)} %bitcast.366) | data formatting | bytes 4194304
  193.1 7.9 %fusion.84 = f32[16,32,256]{2,1,0:T(8,128)S(1)} fusion(f32[16,256]{1,0:T(8,128)S(1)} %get-tuple-element.37, f32[16,256]{1,0:T(8,128)S(1)} %get-tuple-element.38, f32[16,256]{1,0:T(8,128)S(1)} %get-tuple-element.39, f32[16,256]{1,0:T(8,128)S(1)} %sub.778, f32[16,256]{1,0:T(8,128)S(1)} %sub.773, f32[16,256]{1,0:T(8,128)S(1)} %sub.768, ...), kind=kOutput, calls=%fused_computation.93 | convolution fusion | flops 415236096 | bytes 1146880 | tf_op jit(solution)/shard_map/mpq,vmq->vmp/dot_general | solution.py:117
  202.7 7.8 %fusion.139 = f32[16,32,256]{2,1,0:T(8,128)} fusion(f32[16,32,256]{2,1,0:T(8,128)S(1)} %fusion.84, f32[16,256]{1,0:T(8,128)S(1)} %get-tuple-element.41, f32[16,256]{1,0:T(8,128)S(1)} %sub.778, f32[16,256]{1,0:T(8,128)S(1)} %get-tuple-element.42, f32[16,256]{1,0:T(8,128)S(1)} %sub.773, f32[16,256]{1,0:T(8,128)S(1)} %get-tuple-element.43, ...), kind=kOutput, calls=%fused_computation.149 | convolution fusion | flops 415367168 | bytes 1671168 | tf_op jit(solution)/shard_map/mpq,vmq->vmp/dot_general | solution.py:117
  210.4 10.6 %all-to-all-start.3 = ((f32[128,1,384]{2,1,0:T(1,128)}), f32[128,1,384]{2,1,0:T(1,128)S(1)}, u32[]{:S(2)}, u32[]{:S(2)}) async-start(f32[128,1,384]{2,1,0:T(1,128)} %reshape.435), calls=%async_computation.3 | async-start | bytes 393216 | tf_op jit(solution)/shard_map/all_to_all | solution.py:84
  221.2 10.1 %all-to-all-done.3 = f32[128,1,384]{2,1,0:T(1,128)S(1)} async-done(((f32[128,1,384]{2,1,0:T(1,128)}), f32[128,1,384]{2,1,0:T(1,128)S(1)}, u32[]{:S(2)}, u32[]{:S(2)}) %all-to-all-start.3) | async-done | bytes 196640 | tf_op jit(solution)/shard_map/all_to_all | solution.py:84
  239.0 7.2 %all-to-all-done.5 = f32[128,1,384]{2,1,0:T(1,128)S(1)} async-done(((f32[128,1,384]{2,1,0:T(1,128)}), f32[128,1,384]{2,1,0:T(1,128)S(1)}, u32[]{:S(2)}, u32[]{:S(2)}) %all-to-all-start.5) | async-done | bytes 196640 | tf_op jit(solution)/shard_map/all_to_all | solution.py:84
  246.2 5.2 %all-to-all-start = ((f32[128,1,4096]{2,1,0:T(1,128)}), f32[128,1,4096]{2,1,0:T(1,128)}, u32[]{:S(2)}, u32[]{:S(2)}) async-start(f32[128,1,4096]{2,1,0:T(1,128)} %reshape.429), calls=%async_computation | async-start | bytes 4194304 | tf_op jit(solution)/shard_map/all_to_all | solution.py:83
  251.7 8.7 %fusion.142 = f32[16,32,256]{2,1,0:T(8,128)} fusion(f32[16,32,256]{2,1,0:T(8,128)} %fusion.139, f32[16,256]{1,0:T(8,128)S(1)} %get-tuple-element.40, f32[16,256]{1,0:T(8,128)S(1)} %get-tuple-element.36, f32[16,256]{1,0:T(8,128)S(1)} %get-tuple-element.35, f32[16,256]{1,0:T(8,128)S(1)} %sub.778, f32[16,256]{1,0:T(8,128)S(1)} %sub.773, ...), kind=kOutput, calls=%fused_computation.150 | convolution fusion | flops 415367168 | bytes 1671168 | tf_op jit(solution)/shard_map/mpq,vmq->vmp/dot_general | solution.py:117
  263.1 18.7 %all-to-all-done = f32[128,1,4096]{2,1,0:T(1,128)} async-done(((f32[128,1,4096]{2,1,0:T(1,128)}), f32[128,1,4096]{2,1,0:T(1,128)}, u32[]{:S(2)}, u32[]{:S(2)}) %all-to-all-start) | async-done | bytes 2097184 | tf_op jit(solution)/shard_map/all_to_all | solution.py:83
  281.8 5.8 %all-to-all-start.2 = ((f32[128,1,4096]{2,1,0:T(1,128)}), f32[128,1,4096]{2,1,0:T(1,128)}, u32[]{:S(2)}, u32[]{:S(2)}) async-start(f32[128,1,4096]{2,1,0:T(1,128)} %reshape.433), calls=%async_computation.2 | async-start | bytes 4194304 | tf_op jit(solution)/shard_map/all_to_all | solution.py:83
  296.4 8.6 %reduce.12 = f32[128,4096]{1,0:T(8,128)} reduce(f32[128,1,4096]{2,1,0:T(1,128)} %all-to-all-done, f32[]{:T(128)} %broadcast.376), dimensions={1}, to_apply=%all_to_all.18.reduce_sub_computation | reduce | bytes 4194308 | tf_op jit(solution)/shard_map/all_to_all | solution.py:83
  309.8 7.9 %all-to-all-done.2 = f32[128,1,4096]{2,1,0:T(1,128)} async-done(((f32[128,1,4096]{2,1,0:T(1,128)}), f32[128,1,4096]{2,1,0:T(1,128)}, u32[]{:S(2)}, u32[]{:S(2)}) %all-to-all-start.2) | async-done | bytes 2097184 | tf_op jit(solution)/shard_map/all_to_all | solution.py:83
  317.7 5.8 %all-to-all-start.4 = ((f32[128,1,4096]{2,1,0:T(1,128)}), f32[128,1,4096]{2,1,0:T(1,128)}, u32[]{:S(2)}, u32[]{:S(2)}) async-start(f32[128,1,4096]{2,1,0:T(1,128)} %reshape.437), calls=%async_computation.4 | async-start | bytes 4194304 | tf_op jit(solution)/shard_map/all_to_all | solution.py:83
  323.6 21.7 %fusion.30 = f32[128,2,32,64]{3,2,1,0:T(8,128)} fusion(f32[128,2,32,64]{3,2,1,0:T(8,128)} %reshape.430, f32[128,2,64]{2,1,0:T(2,128)} %get-tuple-element.62, f32[128,2,64]{2,1,0:T(2,128)S(1)} %bitcast.399, f32[128,2,64]{2,1,0:T(2,128)} %get-tuple-element.63, f32[128,2,64]{2,1,0:T(2,128)S(1)} %bitcast.398, f32[128,2,64]{2,1,0:T(2,128)S(1)} %get-tuple-element.61, ...), kind=kOutput, calls=%fused_computation.39 | convolution fusion | flops 415236096 | bytes 4587520 | tf_op jit(solution)/shard_map/scij,scvj->scvi/dot_general | solution.py:179
  345.2 5.0 %reshape.318 = f32[256,2048]{1,0:T(8,128)} reshape(f32[128,2,32,64]{3,2,1,0:T(8,128)} %fusion.30) | data formatting | bytes 4194304 | tf_op jit(solution)/shard_map/reshape | solution.py:189
  353.2 8.6 %reduce.14 = f32[128,4096]{1,0:T(8,128)} reduce(f32[128,1,4096]{2,1,0:T(1,128)} %all-to-all-done.2, f32[]{:T(128)} %broadcast.376), dimensions={1}, to_apply=%all_to_all.20.reduce_sub_computation | reduce | bytes 4194308 | tf_op jit(solution)/shard_map/all_to_all | solution.py:83
  366.5 22.0 %fusion.15 = f32[128,2,32,64]{3,2,1,0:T(8,128)} fusion(f32[128,2,32,64]{3,2,1,0:T(8,128)} %reshape.434, f32[128,2,64]{2,1,0:T(2,128)S(1)} %get-tuple-element.59, f32[128,2,64]{2,1,0:T(2,128)S(1)} %bitcast.402, f32[128,2,64]{2,1,0:T(2,128)S(1)} %get-tuple-element.60, f32[128,2,64]{2,1,0:T(2,128)S(1)} %bitcast.401, f32[128,2,64]{2,1,0:T(2,128)S(1)} %get-tuple-element.58, ...), kind=kOutput, calls=%fused_computation.24 | convolution fusion | flops 415236096 | bytes 4587520 | tf_op jit(solution)/shard_map/scij,scvj->scvi/dot_general | solution.py:179
  396.3 8.6 %reduce.16 = f32[128,4096]{1,0:T(8,128)} reduce(f32[128,1,4096]{2,1,0:T(1,128)} %all-to-all-done.4, f32[]{:T(128)} %broadcast.376), dimensions={1}, to_apply=%all_to_all.22.reduce_sub_computation | reduce | bytes 4194308 | tf_op jit(solution)/shard_map/all_to_all | solution.py:83
  409.6 21.7 %fusion = f32[128,2,32,64]{3,2,1,0:T(8,128)} fusion(f32[128,2,32,64]{3,2,1,0:T(8,128)} %reshape.438, f32[128,2,64]{2,1,0:T(2,128)S(1)} %get-tuple-element.56, f32[128,2,64]{2,1,0:T(2,128)S(1)} %bitcast.396, f32[128,2,64]{2,1,0:T(2,128)S(1)} %get-tuple-element.57, f32[128,2,64]{2,1,0:T(2,128)S(1)} %bitcast.395, f32[128,2,64]{2,1,0:T(2,128)S(1)} %get-tuple-element.55, ...), kind=kOutput, calls=%fused_computation.9 | convolution fusion | flops 415236096 | bytes 4587520 | tf_op jit(solution)/shard_map/scij,scvj->scvi/dot_general | solution.py:179
  431.4 5.0 %reshape.324 = f32[256,2048]{1,0:T(8,128)} reshape(f32[128,2,32,64]{3,2,1,0:T(8,128)} %fusion) | data formatting | bytes 4194304 | tf_op jit(solution)/shard_map/reshape | solution.py:189
  (335 shorter events, 193.5 us)
Async XLA Ops:
  1.2 31.8 %copy-start.29 = (f32[3,1792]{1,0:T(4,128)S(1)}, f32[3,1792]{1,0:T(4,128)}, u32[]{:S(2)}) copy-start(f32[3,1792]{1,0:T(4,128)} %param.14) | copy-start | bytes 64516
  8.8 82.6 %collective-permute-start.2 = (f32[32,64]{1,0:T(8,128)}, f32[32,64]{1,0:T(8,128)}, u32[]{:S(2)}, u32[]{:S(2)}) collective-permute-start(f32[32,64]{1,0:T(8,128)} %fusion.307), channel_id=1, source_target_pairs={{0,1},{1,0},{2,3},{3,2},{4,5},{5,4},{6,7},{7,6},{8,9},{9,8},{10,11... | collective-permute-start | bytes 24584 | tf_op jit(solution)/shard_map/ppermute | solution.py:32
  11.2 28.6 %copy-start.34 = (s32[128,2,1]{0,1,2:T(2,128)S(1)}, s32[128,2,1]{0,1,2:T(2,128)}, u32[]{:S(2)}) copy-start(s32[128,2,1]{0,1,2:T(2,128)} %get-tuple-element.80) | copy-start | bytes 3076
  15.3 195.1 %all-to-all-start.1 = ((f32[128,1,384]{2,1,0:T(1,128)}), f32[128,1,384]{2,1,0:T(1,128)S(1)}, u32[]{:S(2)}, u32[]{:S(2)}) async-start(f32[128,1,384]{2,1,0:T(1,128)} %reshape.431), calls=%async_computation.1 | async-start | bytes 393216 | tf_op jit(solution)/shard_map/all_to_all | solution.py:84
  27.3 161.9 %collective-permute-start = (f32[35,256]{1,0:T(8,128)}, f32[35,256]{1,0:T(8,128)}, u32[]{:S(2)}, u32[]{:S(2)}) collective-permute-start(f32[35,256]{1,0:T(8,128)} %get-tuple-element.44), channel_id=1, source_target_pairs={{0,1},{1,2},{2,3},{3,4},{4,5},{5,6},{6,7},{7,8},{8,9},{9,10},{10,1... | collective-permute-start | bytes 107528 | tf_op jit(solution)/shard_map/ppermute | solution.py:19
  30.8 158.4 %collective-permute-start.1 = (f32[35,256]{1,0:T(8,128)}, f32[35,256]{1,0:T(8,128)}, u32[]{:S(2)}, u32[]{:S(2)}) collective-permute-start(f32[35,256]{1,0:T(8,128)} %get-tuple-element.45), channel_id=1, source_target_pairs={{1,0},{2,1},{3,2},{4,3},{5,4},{6,5},{7,6},{8,7},{9,8},{10,9},{11,1... | collective-permute-start | bytes 107528 | tf_op jit(solution)/shard_map/ppermute | solution.py:20
  93.8 6.7 %collective-permute-start.3 = (f32[32,64]{1,0:T(8,128)}, f32[32,64]{1,0:T(8,128)}, u32[]{:S(2)}, u32[]{:S(2)}) collective-permute-start(f32[32,64]{1,0:T(8,128)} %convolution_add_fusion.14), channel_id=1, source_target_pairs={{0,2},{2,0},{1,3},{3,1},{4,6},{6,4},{5,7},{7,5},{8,10},{10,8},{9,1... | collective-permute-start | bytes 24584 | tf_op jit(solution)/shard_map/ppermute | solution.py:32
  102.4 8.0 %collective-permute-start.4 = (f32[32,64]{1,0:T(8,128)S(1)}, f32[32,64]{1,0:T(8,128)S(1)}, u32[]{:S(2)}, u32[]{:S(2)}) collective-permute-start(f32[32,64]{1,0:T(8,128)S(1)} %convolution_add_fusion.12), channel_id=1, source_target_pairs={{0,4},{4,0},{1,5},{5,1},{2,6},{6,2},{3,7},{7,3},{8,12},{12,8},{9,1... | collective-permute-start | bytes 24584 | tf_op jit(solution)/shard_map/ppermute | solution.py:32
  112.1 74.3 %collective-permute-start.5 = (f32[32,64]{1,0:T(8,128)S(1)}, f32[32,64]{1,0:T(8,128)S(1)}, u32[]{:S(2)}, u32[]{:S(2)}) collective-permute-start(f32[32,64]{1,0:T(8,128)S(1)} %convolution_add_fusion.10), channel_id=1, source_target_pairs={{0,8},{8,0},{16,24},{24,16},{32,40},{40,32},{48,56},{56,48},{64,72... | collective-permute-start | bytes 24584 | tf_op jit(solution)/shard_map/ppermute | solution.py:32
  186.7 14.3 %collective-permute-start.6 = (f32[32,64]{1,0:T(8,128)S(1)}, f32[32,64]{1,0:T(8,128)S(1)}, u32[]{:S(2)}, u32[]{:S(2)}) collective-permute-start(f32[32,64]{1,0:T(8,128)S(1)} %convolution_add_fusion.8), channel_id=1, source_target_pairs={{0,16},{16,0},{8,24},{24,8},{32,48},{48,32},{40,56},{56,40},{64,80... | collective-permute-start | bytes 24584 | tf_op jit(solution)/shard_map/ppermute | solution.py:32
  201.4 19.6 %collective-permute-start.7 = (f32[32,64]{1,0:T(8,128)S(1)}, f32[32,64]{1,0:T(8,128)S(1)}, u32[]{:S(2)}, u32[]{:S(2)}) collective-permute-start(f32[32,64]{1,0:T(8,128)S(1)} %convolution_add_fusion.6), channel_id=1, source_target_pairs={{0,32},{32,0},{8,40},{40,8},{16,48},{48,16},{24,56},{56,24},{64,96... | collective-permute-start | bytes 24584 | tf_op jit(solution)/shard_map/ppermute | solution.py:32
  210.4 41.1 %copy-start.4 = (f32[32,16,256]{2,1,0:T(8,128)S(1)}, f32[32,16,256]{2,1,0:T(8,128)}, u32[]{:S(2)}) copy-start(f32[32,16,256]{2,1,0:T(8,128)} %get-tuple-element.32) | copy-start | bytes 1572868
  210.4 20.9 %all-to-all-start.3 = ((f32[128,1,384]{2,1,0:T(1,128)}), f32[128,1,384]{2,1,0:T(1,128)S(1)}, u32[]{:S(2)}, u32[]{:S(2)}) async-start(f32[128,1,384]{2,1,0:T(1,128)} %reshape.435), calls=%async_computation.3 | async-start | bytes 393216 | tf_op jit(solution)/shard_map/all_to_all | solution.py:84
  231.3 14.9 %all-to-all-start.5 = ((f32[128,1,384]{2,1,0:T(1,128)}), f32[128,1,384]{2,1,0:T(1,128)S(1)}, u32[]{:S(2)}, u32[]{:S(2)}) async-start(f32[128,1,384]{2,1,0:T(1,128)} %reshape.439), calls=%async_computation.5 | async-start | bytes 393216 | tf_op jit(solution)/shard_map/all_to_all | solution.py:84
  236.0 24.5 %collective-permute-start.8 = (f32[32,64]{1,0:T(8,128)S(1)}, f32[32,64]{1,0:T(8,128)}, u32[]{:S(2)}, u32[]{:S(2)}) collective-permute-start(f32[32,64]{1,0:T(8,128)S(1)} %convolution_add_fusion.4), channel_id=1, source_target_pairs={{0,64},{64,0},{8,72},{72,8},{16,80},{80,16},{24,88},{88,24},{32,96... | collective-permute-start | bytes 24584 | tf_op jit(solution)/shard_map/ppermute | solution.py:32
  246.2 35.5 %all-to-all-start = ((f32[128,1,4096]{2,1,0:T(1,128)}), f32[128,1,4096]{2,1,0:T(1,128)}, u32[]{:S(2)}, u32[]{:S(2)}) async-start(f32[128,1,4096]{2,1,0:T(1,128)} %reshape.429), calls=%async_computation | async-start | bytes 4194304 | tf_op jit(solution)/shard_map/all_to_all | solution.py:83
  260.5 27.8 %copy-start.41 = (f32[64]{0:T(128)S(1)}, f32[64]{0:T(128)}, u32[]{:S(2)}) copy-start(f32[64]{0:T(128)} %get-tuple-element.94) | copy-start | bytes 772
  260.5 27.8 %copy-start.42 = (f32[64]{0:T(128)S(1)}, f32[64]{0:T(128)}, u32[]{:S(2)}) copy-start(f32[64]{0:T(128)} %get-tuple-element.95) | copy-start | bytes 772
  260.5 27.8 %copy-start.43 = (f32[64]{0:T(128)S(1)}, f32[64]{0:T(128)}, u32[]{:S(2)}) copy-start(f32[64]{0:T(128)} %get-tuple-element.96) | copy-start | bytes 772
  260.5 27.8 %copy-start.44 = (f32[64]{0:T(128)S(1)}, f32[64]{0:T(128)}, u32[]{:S(2)}) copy-start(f32[64]{0:T(128)} %get-tuple-element.148) | copy-start | bytes 772
  260.5 28.8 %copy-start.6 = (f32[1,64,64]{2,1,0:T(8,128)S(1)}, f32[1,64,64]{2,1,0:T(8,128)}, u32[]{:S(2)}) copy-start(f32[1,64,64]{2,1,0:T(8,128)} %copy.194) | copy-start | bytes 49156
  260.5 28.9 %copy-start.72 = (f32[64]{0:T(128)S(1)}, f32[64]{0:T(128)}, u32[]{:S(2)}) copy-start(f32[64]{0:T(128)} %get-tuple-element.88) | copy-start | bytes 772
  281.8 35.9 %all-to-all-start.2 = ((f32[128,1,4096]{2,1,0:T(1,128)}), f32[128,1,4096]{2,1,0:T(1,128)}, u32[]{:S(2)}, u32[]{:S(2)}) async-start(f32[128,1,4096]{2,1,0:T(1,128)} %reshape.433), calls=%async_computation.2 | async-start | bytes 4194304 | tf_op jit(solution)/shard_map/all_to_all | solution.py:83
  317.7 78.6 %all-to-all-start.4 = ((f32[128,1,4096]{2,1,0:T(1,128)}), f32[128,1,4096]{2,1,0:T(1,128)}, u32[]{:S(2)}, u32[]{:S(2)}) async-start(f32[128,1,4096]{2,1,0:T(1,128)} %reshape.437), calls=%async_computation.4 | async-start | bytes 4194304 | tf_op jit(solution)/shard_map/all_to_all | solution.py:83
  (70 other events, 986.7 us)
where the time goes:
time: 457 us; the launch traced here: 450 us
  local copies, waits for them, and re-layouts  191 us (42%)
  matrix products  117 us (26%)
  starting transfers between devices  61.5 us (13%)
  waiting for transfers between devices  44 us (10%)
  other arithmetic  34.2 us (7%)
    unnamed x187, local copies, waits for them, and re-layouts  85.3 us
    dot_general x3, matrix products, on_device(): jnp.einsum('scij,scvj->scvi', kernel_list, got_coefs, precision=PRECISE)  65.3 us
    dynamic_slice x1, local copies, waits for them, and re-layouts, climb(): lax.dynamic_index_in_dim(up_transfer, offset + node_id, 0, keepdims=False)  30.6 us
    all_to_all x3, waiting for transfers between devices, route_blocks(): lax.all_to_all(send_coefs, ('leaf', 'pts'), split_axis=0, concat_axis=0,...  26.6 us
    all_to_all x3, other arithmetic, route_blocks(): lax.all_to_all(send_coefs, ('leaf', 'pts'), split_axis=0, concat_axis=0,...  25.9 us
    all_to_all x3, starting transfers between devices, route_blocks(): lax.all_to_all(send_points, ('leaf', 'pts'), split_axis=0, concat_axis=0,...  25.3 us
    dot_general x3, matrix products, on_device(): jnp.einsum('mpq,vmq->vmp', kernel, near_block[:vec_count], precision=PREC...  24.3 us
    all_to_all x3, waiting for transfers between devices, route_blocks(): lax.all_to_all(send_points, ('leaf', 'pts'), split_axis=0, concat_axis=0,...  17.4 us
  transfers between devices with their start and end apart: 15, of which 4 were waited for; matrix products, arithmetic and copies ran while one was open for 62% of the time, Pallas kernels for 0%

commit v1 on v0

v1 whole, which is shorter than its diff:
```python
import functools
import math

import jax
import jax.numpy as jnp
from jax import lax
from jax.experimental import pallas as pl
from jax.experimental.pallas import tpu as pltpu
from jax.sharding import PartitionSpec as P

F32 = jnp.float32
BF16 = jnp.bfloat16
MESH = pl.DeviceIdType.MESH
LN2 = math.log(2.0)
KAPPA = math.sqrt(3.0) / 0.3 / LN2
TINY = 1e-30

VEC = 32
RANK = 64
LEAF = 256
LEAVES = 16
PTS = 8
LEAFS = 16
PAIRS = 14
NODES = 28
COEF_ROWS = PAIRS * VEC
PAY_ROWS = COEF_ROWS + PAIRS * 8
UPPER = 7
NN = (((1,), (0,)), ((), ()))
NT = (((1,), (1,)), ((), ()))


def dg(a, b, dims):
    return lax.dot_general(a, b, dims, preferred_element_type=F32)


def split(x):
    hi = x.astype(BF16)
    return hi, (x - hi.astype(F32)).astype(BF16)


def dot3(a, b, dims):
    ah, al = split(a)
    bh, bl = split(b)
    return dg(ah, bh, dims) + (dg(ah, bl, dims) + dg(al, bh, dims))


def split3(x):
    h = x.astype(BF16).astype(F32)
    r = x - h
    m = r.astype(BF16).astype(F32)
    return h, m, r - m


def forms(pts):
    n = pts.shape[1]
    x = (pts - 0.5) * KAPPA
    x = jnp.concatenate([x, jnp.zeros((5, n), F32)], axis=0)
    q = jnp.sum(x * x, axis=0, keepdims=True)
    row = lax.broadcasted_iota(jnp.int32, (8, n), 0)
    w = jnp.where(row < 3, x, jnp.where(row == 3, 1.0, jnp.where(row == 4, q, 0.0)))
    u = jnp.where(row < 3, -2.0 * x, jnp.where(row == 3, q, jnp.where(row == 4, 1.0, 0.0)))
    return u, w


def stack_u(u):
    h, m, l = split3(u)
    z = jnp.zeros_like(h)
    return jnp.concatenate([h, h, m, m, h, l, z, z], axis=0)


def stack_w(w):
    h, m, l = split3(w)
    z = jnp.zeros_like(h)
    return jnp.concatenate([h, m, h, m, l, h, z, z], axis=0)


def matern(squared):
    squared = jnp.maximum(squared, TINY)
    t = squared * lax.rsqrt(squared)
    return (1.0 + LN2 * t) * jnp.exp2(-t)


def pair_matrix(lt_ref, n):
    return jnp.concatenate([lt_ref[2 * n], lt_ref[2 * n + 1]], axis=1)


def up_offset(u):
    return 0 if u == 0 else 256 - (128 >> (u - 1))


def gather_kernel(
    vec_ref, pts_ref, base_ref, lt_ref, skel_ref, upt_ref, upp_ref, sc_ref, tc_ref,
    g_ref, near_ref, far_ref, tp_ref, scg_ref, tcg_ref,
    u_scr, w_scr, v_scr, halo_src, halo_dst, pay, tpay, ut, xs, xr, sf,
    ssem, rsem, lsem,
):
    leaf = lax.axis_index("leaf")
    p = lax.axis_index("pts")
    me = leaf * PTS + p
    y = leaf // 4
    z = lax.rem(leaf, 4)
    nxt = lax.rem(me + 1, 128)
    prv = lax.rem(me + 127, 128)
    nxt_dev = (nxt // PTS, lax.rem(nxt, PTS))
    prv_dev = (prv // PTS, lax.rem(prv, PTS))

    barrier = pltpu.get_barrier_semaphore()
    for k in range(1, LEAFS):
        pl.semaphore_signal(barrier, inc=1, device_id=(leaf ^ k, p), device_id_type=MESH)
    for k in range(1, PTS):
        pl.semaphore_signal(barrier, inc=1, device_id=(leaf, p ^ k), device_id_type=MESH)
    pl.semaphore_signal(barrier, inc=1, device_id=nxt_dev, device_id_type=MESH)
    pl.semaphore_signal(barrier, inc=1, device_id=prv_dev, device_id_type=MESH)

    counter = [0]
    sends = []

    def remote(src, dst, dev):
        i = counter[0]
        counter[0] += 1
        copy = pltpu.make_async_remote_copy(
            src_ref=src, dst_ref=dst, send_sem=ssem.at[i], recv_sem=rsem.at[i],
            device_id=dev, device_id_type=MESH,
        )
        copy.start()
        sends.append(copy)
        return copy

    locals_ = []

    def local(src, dst):
        copy = pltpu.make_async_copy(src, dst, lsem.at[len(locals_)])
        copy.start()
        locals_.append(copy)

    for u in range(UPPER):
        first = lax.shift_right_logical(me, u + 1) * 2
        local(upt_ref.at[pl.ds(up_offset(u) + first, 2)], ut.at[u])

    for side, off in ((0, 0), (1, (LEAVES - 1) * LEAF)):
        halo_src[side, 0:VEC] = vec_ref[:, off:off + LEAF]
        halo_src[side, VEC:VEC + 8] = jnp.concatenate(
            [pts_ref[:, off:off + LEAF], jnp.zeros((5, LEAF), F32)], axis=0
        )
    for a in range(PAIRS):
        u8, w8 = forms(skel_ref[:, a * 128:(a + 1) * 128])
        tpay[a * 8:(a + 1) * 8] = u8
        pay[COEF_ROWS + a * 8:COEF_ROWS + (a + 1) * 8] = w8

    pl.semaphore_wait(barrier, LEAFS + PTS)

    h0 = remote(halo_src.at[0], halo_dst.at[1], prv_dev)
    h1 = remote(halo_src.at[1], halo_dst.at[0], nxt_dev)
    arrivals = []
    for k in range(1, PTS):
        arrivals.append(remote(tpay, tp_ref.at[p], (leaf, p ^ k)))
        arrivals.append(remote(tc_ref, tcg_ref.at[p], (leaf, p ^ k)))
    for k in range(1, LEAFS):
        arrivals.append(remote(sc_ref, scg_ref.at[leaf], (leaf ^ k, p)))
    local(tpay, tp_ref.at[p])
    local(tc_ref, tcg_ref.at[p])
    local(sc_ref, scg_ref.at[leaf])

    pairs = []
    for m in range(LEAVES // 2):
        both = []
        for j in range(2):
            n = 2 * m + j
            both.append(dot3(vec_ref[:, n * LEAF:(n + 1) * LEAF], base_ref[n], NT))
        pairs.append(jnp.concatenate(both, axis=1))
    base = 0
    row = 0
    root = None
    while True:
        if row < COEF_ROWS:
            for c in pairs:
                pay[row:row + VEC] = c
                row += VEC
        ups = [dot3(c, pair_matrix(lt_ref, base + i), NT) for i, c in enumerate(pairs)]
        base += len(pairs)
        if len(ups) == 1:
            root = ups[0]
            break
        pairs = [
            jnp.concatenate([ups[2 * i], ups[2 * i + 1]], axis=1) for i in range(len(ups) // 2)
        ]

    half = PAY_ROWS // 2
    quarter = 136

    def lid(yy, zz):
        return lax.rem(yy + 4, 4) * 4 + lax.rem(zz + 4, 4)

    def near_id(h, stage, step):
        return lid(y, z + step) if (h == 0) == (stage == 0) else lid(y + step, z)

    def block_id(h, first, second):
        return lid(y + second, z + first) if h == 0 else lid(y + first, z + second)

    stage1 = {}
    stage2 = {}
    for h in range(2):
        rows = pl.ds(h * half, half)
        for step in (1, -1):
            stage1[h, step] = remote(
                pay.at[rows], g_ref.at[leaf, rows], (near_id(h, 0, step), p)
            )

    def spread(h, first):
        rows = pl.ds(h * half, half)
        blk = near_id(h, 0, first)
        src = pay.at[rows] if first == 0 else g_ref.at[blk, rows]
        for step in (1, -1):
            stage2[h, first, step] = remote(
                src, g_ref.at[blk, rows], (near_id(h, 1, step), p)
            )

    for h in range(2):
        spread(h, 0)
    local(pay, g_ref.at[leaf])

    def forward(h, stage, blk_minus, blk_plus, got_minus, got_plus):
        got_minus.wait_recv()
        rows = pl.ds(h * half, quarter)
        one = remote(g_ref.at[blk_minus, rows], g_ref.at[blk_minus, rows], (near_id(h, stage, 1), p))
        got_plus.wait_recv()
        rows = pl.ds(h * half + quarter, half - quarter)
        two = remote(g_ref.at[blk_plus, rows], g_ref.at[blk_plus, rows], (near_id(h, stage, -1), p))
        return one, two

    opposite = {}

    def step_a():
        for h in range(2):
            opposite[h] = forward(
                h, 0, near_id(h, 0, -1), near_id(h, 0, 1), stage1[h, 1], stage1[h, -1]
            )
            spread(h, -1)
            spread(h, 1)

    def step_b():
        for h in range(2):
            opposite[h][0].wait_recv()
            opposite[h][1].wait_recv()
            spread(h, 2)

    last = []

    def step_c(first):
        for h in range(2):
            last.extend(
                forward(
                    h, 1, block_id(h, first, -1), block_id(h, first, 1),
                    stage2[h, first, 1], stage2[h, first, -1],
                )
            )

    upward = {}

    def send_up(u, value):
        xs[u] = value
        dev = (leaf, p ^ (1 << u)) if u < 3 else (leaf ^ (1 << (u - 3)), p)
        upward[u] = remote(xs.at[u], xr.at[u], dev)

    send_up(0, root)

    def climb(u):
        upward[u].wait_recv()
        locals_[u].wait()
        node = lax.shift_right_logical(me, u)
        left_side = lax.rem(node, 2) == 0
        own = xs[u]
        sib = xr[u]
        pair = jnp.concatenate(
            [jnp.where(left_side, own, sib), jnp.where(left_side, sib, own)], axis=1
        )
        if u < UPPER - 1:
            mat = jnp.concatenate([ut[u, 0], ut[u, 1]], axis=1)
            send_up(u + 1, dot3(pair, mat, NT))
        col = pl.multiple_of((up_offset(u) + (node // 2) * 2) * RANK, 128)
        u8, w8 = forms(upp_ref[:, pl.ds(col, 128)])
        kern = matern(dg(stack_u(u8).T.astype(BF16), stack_w(w8).astype(BF16), NN))
        lane_left = lax.broadcasted_iota(jnp.int32, (VEC, 2 * RANK), 1) < RANK
        only_sib = jnp.where(jnp.logical_xor(lane_left, left_side), pair, 0.0)
        out = dot3(only_sib, kern, NN)
        sf[u] = jnp.where(left_side, out[:, :RANK], out[:, RANK:])

    def prepare(slot, vec, pts):
        vh, vl = split(vec)
        lanes = pl.ds(pl.multiple_of(slot * LEAF, LEAF), LEAF)
        v_scr[0:VEC, lanes] = vh
        v_scr[VEC:2 * VEC, lanes] = vl
        u8, w8 = forms(pts)
        w_scr[:, lanes] = stack_w(w8).astype(BF16)
        u_scr[lanes, :] = stack_u(u8).T.astype(BF16)

    @pl.loop(0, LEAVES)
    def _(m):
        lanes = pl.ds(pl.multiple_of(m * LEAF, LEAF), LEAF)
        prepare(m + 1, vec_ref[:, lanes], pts_ref[:, lanes])

    def near(m):
        lanes = pl.ds(pl.multiple_of(m * LEAF, LEAF), LEAF)
        w = w_scr[:, lanes]
        total = None
        for b in range(3):
            src = pl.ds(pl.multiple_of((m - 1 + b) * LEAF, LEAF), LEAF)
            kh, kl = split(matern(dg(u_scr[src, :], w, NN)))
            v = v_scr[:, src]
            big = dg(v, kh, NN)
            part = big[:VEC] + (big[VEC:] + dg(v[:VEC], kl, NN))
            total = part if total is None else total + part
        near_ref[:, pl.ds(pl.multiple_of((m - 1) * LEAF, LEAF), LEAF)] = total

    def near_span(lo, hi):
        @pl.loop(lo, hi)
        def _(m):
            near(m)

    step_a()
    climb(0)
    near_span(2, 3)
    climb(1)
    near_span(3, 4)
    step_b()
    climb(2)
    near_span(4, 6)
    step_c(0)
    climb(3)
    near_span(6, 8)
    climb(4)
    near_span(8, 10)
    step_c(-1)
    climb(5)
    near_span(10, 12)
    step_c(1)
    climb(6)
    near_span(12, 14)
    step_c(2)
    near_span(14, 16)
    h0.wait_recv()
    h1.wait_recv()
    for side, slot, edge in ((0, 0, 0), (1, LEAVES + 1, 127)):
        vec = jnp.where(me == edge, 0.0, halo_dst[side, 0:VEC])
        prepare(slot, vec, halo_dst[side, VEC:VEC + 3])
    near(1)
    near(LEAVES)

    far = sf[UPPER - 1]
    for u in range(UPPER - 2, -1, -1):
        left_side = lax.rem(lax.shift_right_logical(me, u), 2) == 0
        mat = jnp.where(left_side, ut[u, 0], ut[u, 1])
        far = sf[u] + dot3(far, mat, NN)
    far_ref[...] = far

    for c in arrivals:
        c.wait_recv()
    for c in last:
        c.wait_recv()
    for c in sends:
        c.wait_send()
    for c in locals_[UPPER:]:
        c.wait()


def couple_kernel(g_ref, tp_ref, sc_ref, tc_ref, o_ref, ca, cb, wa, wb, ua, ub, acc_a, acc_b):
    leaf = lax.axis_index("leaf")
    p = lax.axis_index("pts")
    low = lax.broadcasted_iota(jnp.int32, (VEC, 128), 1) < RANK
    low_w = lax.broadcasted_iota(jnp.int32, (64, 128), 1) < RANK

    @pl.loop(0, LEAFS)
    def _(s):
        for a in range(PAIRS):
            c = g_ref[s, a * VEC:(a + 1) * VEC, :]
            h = c.astype(BF16).astype(F32)
            l = c - h
            node = s * NODES + 2 * a
            w = stack_w(g_ref[s, COEF_ROWS + a * 8:COEF_ROWS + (a + 1) * 8, :])
            wr = pltpu.roll(w, RANK, 1)
            for j in range(2):
                rows = pl.ds(pl.multiple_of((node + j) * 64, 64), 64)
                cur, oth = (w, wr) if j == 0 else (wr, w)
                wa[rows, :] = jnp.where(low_w, cur, 0.0).astype(BF16)
                wb[rows, :] = jnp.where(low_w, 0.0, oth).astype(BF16)
            x = jnp.concatenate([h, l], axis=0)
            xr = pltpu.roll(x, RANK, 1)
            for j in range(2):
                rows = pl.ds(pl.multiple_of((node + j) * 64, 64), 64)
                cur, oth = (x, xr) if j == 0 else (xr, x)
                ca[rows, :] = jnp.where(low_w, cur, 0.0).astype(BF16)
                cb[rows, :] = jnp.where(low_w, 0.0, oth).astype(BF16)

    @pl.loop(0, PTS)
    def _(d):
        zero = jnp.zeros((64, 64), F32)
        for a in range(PAIRS):
            t = stack_u(tp_ref[d, a * 8:(a + 1) * 8, :]).T
            for j in range(2):
                rows = pl.ds(pl.multiple_of((d * 32 + 2 * a + j) * 64, 64), 64)
                part = t[j * 64:(j + 1) * 64]
                ua[rows, :] = jnp.concatenate([part, zero], axis=1).astype(BF16)
                ub[rows, :] = jnp.concatenate([zero, part], axis=1).astype(BF16)
        rows = pl.ds(pl.multiple_of((d * 32 + NODES) * 64, 64), 64)
        ua[rows, :] = jnp.zeros((64, 128), BF16)
        ub[rows, :] = jnp.zeros((64, 128), BF16)
        rows = pl.ds(pl.multiple_of(d * 32 * VEC, 32), 32 * VEC)
        acc_a[rows, :] = jnp.zeros((32 * VEC, RANK), F32)
        acc_b[rows, :] = jnp.zeros((32 * VEC, RANK), F32)

    @pl.loop(0, PTS * 3)
    def _(g):
        d = g // 3
        lev = lax.rem(g, 3)
        outs = []
        for s in range(LEAFS):
            na = s * NODES + sc_ref[s, lev * 2, leaf * PTS + d]
            nb = s * NODES + sc_ref[s, lev * 2 + 1, leaf * PTS + d]
            ra = d * 32 + tc_ref[d, lev * 2, s * PTS + p]
            rb = d * 32 + tc_ref[d, lev * 2 + 1, s * PTS + p]
            na = pl.multiple_of(na * 64, 64)
            nb = pl.multiple_of(nb * 64, 64)
            u = ua[pl.ds(pl.multiple_of(ra * 64, 64), 64), :] + ub[pl.ds(pl.multiple_of(rb * 64, 64), 64), :]
            w = jnp.concatenate([wa[pl.ds(na, 64), :], wb[pl.ds(nb, 64), :]], axis=0)
            kh, kl = split(matern(dg(u, w, NN)))
            xa = ca[pl.ds(na, 64), :]
            xb = cb[pl.ds(nb, 64), :]
            one = dg(jnp.concatenate([xa, xb], axis=0), kh, NT)
            two = dg(jnp.concatenate([xa[:VEC], xb[:VEC]], axis=0), kl, NT)
            outs.append((
                ra, rb,
                one[0:32] + (one[32:64] + two[0:32]),
                one[64:96] + (one[96:128] + two[32:64]),
            ))
        for ra, rb, pa, pb in outs:
            acc_a[pl.ds(pl.multiple_of(ra * VEC, VEC), VEC), :] += pa
            acc_b[pl.ds(pl.multiple_of(rb * VEC, VEC), VEC), :] += pb

    @pl.loop(0, PTS)
    def _(d):
        for a in range(PAIRS):
            both = []
            for j in range(2):
                rows = pl.ds(pl.multiple_of((d * 32 + 2 * a + j) * VEC, VEC), VEC)
                both.append(acc_a[rows, :] + acc_b[rows, :])
            o_ref[d, a * VEC:(a + 1) * VEC, :] = jnp.concatenate(both, axis=1)


def scatter_kernel(acc_ref, far_ref, lt_ref, base_ref, near_ref, out_ref, from_core, s1, s2, work, ssem, rsem):
    leaf = lax.axis_index("leaf")
    p = lax.axis_index("pts")
    x = p // 2
    core = lax.rem(p, 2)
    sister = (leaf, p ^ 1)

    def dev(step):
        return (leaf, lax.rem(x + step + 4, 4) * 2 + core)

    barrier = pltpu.get_barrier_semaphore()
    for d in (sister, dev(1), dev(-1)):
        pl.semaphore_signal(barrier, inc=1, device_id=d, device_id_type=MESH)
    pl.semaphore_wait(barrier, 3)

    sends = []

    def remote(src, dst, device):
        i = len(sends)
        copy = pltpu.make_async_remote_copy(
            src_ref=src, dst_ref=dst, send_sem=ssem.at[i], recv_sem=rsem.at[i],
            device_id=device, device_id_type=MESH,
        )
        copy.start()
        sends.append(copy)
        return copy

    half = COEF_ROWS // 2
    steps = (2, 1, 3, 0)
    first = {}
    for st in steps:
        xx = lax.rem(x + st, 4)
        first[st] = remote(acc_ref.at[xx * 2 + 1 - core], from_core.at[st], sister)

    def summed(st):
        first[st].wait_recv()
        return acc_ref[lax.rem(x + st, 4) * 2 + core] + from_core[st]

    work[0] = summed(2)
    a1 = remote(work.at[0, pl.ds(0, half)], s1.at[pl.ds(0, half)], dev(1))
    b1 = remote(work.at[0, pl.ds(half, half)], s1.at[pl.ds(half, half)], dev(-1))
    work[1] = summed(1)
    work[2] = summed(3)
    a1.wait_recv()
    work[1, 0:half] += s1[0:half]
    a2 = remote(work.at[1], s2.at[0], dev(1))
    b1.wait_recv()
    work[2, half:] += s1[half:]
    b2 = remote(work.at[2], s2.at[1], dev(-1))

    def down(node, n):
        return dot3(node, pair_matrix(lt_ref, n), NN)

    top = down(far_ref[...], 14)
    level2 = [down(top[:, :RANK], 12), down(top[:, RANK:], 13)]
    own = summed(0)
    a2.wait_recv()
    b2.wait_recv()
    work[3] = own + (s2[0] + s2[1])

    def coupling(a):
        return work[3, a * VEC:(a + 1) * VEC]

    pairs = [level2[i] + coupling(12 + i) for i in range(2)]
    pairs = [
        down(pairs[i // 2][:, (i % 2) * RANK:(i % 2 + 1) * RANK], 8 + i) + coupling(8 + i)
        for i in range(4)
    ]
    pairs = [
        down(pairs[i // 2][:, (i % 2) * RANK:(i % 2 + 1) * RANK], i) + coupling(i)
        for i in range(8)
    ]
    for m in range(LEAVES):
        c = pairs[m // 2][:, (m % 2) * RANK:(m % 2 + 1) * RANK]
        cols = slice(m * LEAF, (m + 1) * LEAF)
        out_ref[:, cols] = near_ref[:, cols] + dot3(c, base_ref[m], NN)
    for c in sends:
        c.wait_send()


def vmem():
    return pl.BlockSpec(memory_space=pltpu.VMEM)


def smem():
    return pl.BlockSpec(memory_space=pltpu.SMEM)


def anywhere():
    return pl.BlockSpec(memory_space=pl.ANY)


def shape(*dims, dtype=F32):
    return jax.ShapeDtypeStruct(dims, dtype)


def on_device(
    vectors, points, leaf_bases, local_transfer, skel_points, up_transfer, up_points,
    source_ids, target_ids, live_counts,
):
    me = lax.axis_index("leaf") * PTS + lax.axis_index("pts")
    counts = jnp.array([LEAVES, LEAVES // 2, LEAVES // 4], jnp.int32)
    starts = jnp.array([0, LEAVES, LEAVES + LEAVES // 2], jnp.int32)
    shift = (starts - me * counts)[:, None, None]
    slot = jnp.arange(2, dtype=jnp.int32)
    source_code = jnp.swapaxes(source_ids[:, 0], 1, 2) + shift
    target_code = jnp.where(
        slot[None, :, None] < live_counts[:, 0, None, :],
        jnp.swapaxes(target_ids[:, 0], 1, 2) + shift,
        NODES,
    )
    source_code = jnp.pad(source_code.reshape(6, 128), ((0, 2), (0, 0)))
    target_code = jnp.pad(target_code.reshape(6, 128), ((0, 2), (0, 0)))
    lt = local_transfer[0]
    n_remote = 96

    gathered, near, far, tp, scg, tcg = pl.pallas_call(
        gather_kernel,
        out_shape=(
            shape(LEAFS, PAY_ROWS, 128), shape(VEC, LEAVES * LEAF), shape(VEC, RANK),
            shape(PTS, PAIRS * 8, 128), shape(LEAFS, 8, 128, dtype=jnp.int32),
            shape(PTS, 8, 128, dtype=jnp.int32),
        ),
        in_specs=[vmem()] * 5 + [anywhere()] + [vmem()] * 3,
        out_specs=(vmem(),) * 6,
        scratch_shapes=[
            pltpu.VMEM((18 * LEAF, 64), BF16),
            pltpu.VMEM((64, 18 * LEAF), BF16),
            pltpu.VMEM((2 * VEC, 18 * LEAF), BF16),
            pltpu.VMEM((2, VEC + 8, LEAF), F32),
            pltpu.VMEM((2, VEC + 8, LEAF), F32),
            pltpu.VMEM((PAY_ROWS, 128), F32),
            pltpu.VMEM((PAIRS * 8, 128), F32),
            pltpu.VMEM((UPPER, 2, RANK, RANK), F32),
            pltpu.VMEM((UPPER, VEC, RANK), F32),
            pltpu.VMEM((UPPER, VEC, RANK), F32),
            pltpu.VMEM((UPPER, VEC, RANK), F32),
            pltpu.SemaphoreType.DMA((n_remote,)),
            pltpu.SemaphoreType.DMA((n_remote,)),
            pltpu.SemaphoreType.DMA((16,)),
        ],
        compiler_params=pltpu.CompilerParams(
            collective_id=0, has_side_effects=True, vmem_limit_bytes=48 << 20
        ),
    )(vectors, points, leaf_bases, lt, skel_points, up_transfer, up_points, source_code, target_code)

    partial = pl.pallas_call(
        couple_kernel,
        out_shape=shape(PTS, COEF_ROWS, 128),
        in_specs=[vmem(), vmem(), smem(), smem()],
        out_specs=vmem(),
        scratch_shapes=[
            pltpu.VMEM((LEAFS * NODES * 64, 128), BF16),
            pltpu.VMEM((LEAFS * NODES * 64, 128), BF16),
            pltpu.VMEM((LEAFS * NODES * 64, 128), BF16),
            pltpu.VMEM((LEAFS * NODES * 64, 128), BF16),
            pltpu.VMEM((PTS * 32 * 64, 128), BF16),
            pltpu.VMEM((PTS * 32 * 64, 128), BF16),
            pltpu.VMEM((PTS * 32 * VEC, RANK), F32),
            pltpu.VMEM((PTS * 32 * VEC, RANK), F32),
        ],
        compiler_params=pltpu.CompilerParams(vmem_limit_bytes=56 << 20),
    )(gathered, tp, scg, tcg)

    return pl.pallas_call(
        scatter_kernel,
        out_shape=shape(VEC, LEAVES * LEAF),
        in_specs=[vmem()] * 5,
        out_specs=vmem(),
        scratch_shapes=[
            pltpu.VMEM((4, COEF_ROWS, 128), F32),
            pltpu.VMEM((COEF_ROWS, 128), F32),
            pltpu.VMEM((2, COEF_ROWS, 128), F32),
            pltpu.VMEM((4, COEF_ROWS, 128), F32),
            pltpu.SemaphoreType.DMA((8,)),
            pltpu.SemaphoreType.DMA((8,)),
        ],
        compiler_params=pltpu.CompilerParams(
            collective_id=1, has_side_effects=True, vmem_limit_bytes=48 << 20
        ),
    )(partial, far, lt, leaf_bases, near)


def solution(mesh):
    both = ("leaf", "pts")
    return jax.shard_map(
        on_device,
        mesh=mesh,
        in_specs=(
            P(None, both),
            P(None, both),
            P(both, None, None),
            P(both, None, None, None),
            P(None, both),
            P(),
            P(),
            P(None, both, None, None),
            P(None, both, None, None),
            P(None, both, None),
        ),
        out_specs=P(None, both),
        check_vma=False,
    )
```

time: 457 us -> 136 us (0.30); the launches traced: 450 us -> 136 us
  local copies, waits for them, and re-layouts: 191 us -> 13.3 us
  Pallas kernels: 0 us -> 120 us
  matrix products: 117 us -> 0 us
  starting transfers between devices: 61.5 us -> 0 us
  waiting for transfers between devices: 44 us -> 0 us
  other arithmetic: 34.2 us -> 2.18 us
    pallas_call x0 -> x3, Pallas kernels: none -> 120 us  [the longest x1 52.7 us: on_device(): pl.pallas_call(couple_kernel, out_shape=shape(PTS, COEF_ROWS, 128), in_sp...]
    dot_general x44 -> x0, matrix products: 117 us -> none  [the longest x3 65.3 us: on_device(): jnp.einsum('scij,scvj->scvi', kernel_list, got_coefs, precision=PRECISE)]
    unnamed x187 -> x23, local copies, waits for them, and re-layouts: 85.3 us -> 13.2 us
    all_to_all x6 -> x0, waiting for transfers between devices: 44 us -> none  [the longest x3 26.6 us: route_blocks(): lax.all_to_all(send_coefs, ('leaf', 'pts'), split_axis=0, concat_axis=0,...]
    all_to_all x6 -> x0, starting transfers between devices: 42.2 us -> none  [the longest x3 25.3 us: route_blocks(): lax.all_to_all(send_points, ('leaf', 'pts'), split_axis=0, concat_axis=0,...]
    dynamic_slice x2 -> x0, local copies, waits for them, and re-layouts: 31.6 us -> none  [the longest x1 30.6 us: climb(): lax.dynamic_index_in_dim(up_transfer, offset + node_id, 0, keepdims=False)]
    all_to_all x6 -> x0, other arithmetic: 29.1 us -> none  [the longest x3 25.9 us: route_blocks(): lax.all_to_all(send_coefs, ('leaf', 'pts'), split_axis=0, concat_axis=0,...]
    gather x12 -> x0, local copies, waits for them, and re-layouts: 22.4 us -> none  [the longest x3 9.25 us: on_device(): send_coef_list.append(coefficients[height][sources])]
  transfers between devices with their start and end apart: 15 -> 0, of which waited for: 4 -> 0; matrix products, arithmetic and copies ran while one was open for 62% -> 0% of each run, Pallas kernels for 0% -> 0%
where the time goes in v1:
time: 136 us
  Pallas kernels  120 us (88%)
  local copies, waits for them, and re-layouts  13.3 us (10%)
  other arithmetic  2.18 us (2%)
    pallas_call x1, Pallas kernels, on_device(): pl.pallas_call(couple_kernel, out_shape=shape(PTS, COEF_ROWS, 128), in_sp...  52.7 us
    pallas_call x1, Pallas kernels, on_device(): pl.pallas_call(gather_kernel, out_shape=(shape(LEAFS, PAY_ROWS, 128), sha...  47.1 us
    pallas_call x1, Pallas kernels, on_device(): pl.pallas_call(scatter_kernel, out_shape=shape(VEC, LEAVES * LEAF), in_sp...  20.4 us
    unnamed x23, local copies, waits for them, and re-layouts  13.2 us

profile of v1, /device:TPU:1, one launch (start us, length us, event | category | flops | bytes accessed | tf_op | source)
XLA Modules:
  0.0 135.8 jit_solution(4183198202448139044)
XLA Ops:
  0.0 0.7 multiply_subtract_fusion
  0.7 0.7 copy.16
  1.4 0.8 compare_select_fusion
  2.1 0.8 fusion
  2.9 0.0 copy-start.2
  2.9 0.0 copy-start.3
  2.9 0.0 copy-start.5
  2.9 0.0 copy-start.6
  3.0 0.0 copy-start.9
  3.0 8.2 %copy.13.upt_ref = f32[254,64,64]{2,1,0:T(8,128)} copy(f32[254,64,64]{0,2,1:T(8,128)} %param.17) | data formatting | bytes 8323072 | tf_op args[5]
  11.2 0.0 copy-done.1
  11.2 0.0 copy-done.2
  11.2 0.0 copy-done.5
  11.2 0.0 copy-done.6
  11.2 0.0 copy-done.9
  11.3 47.1 %shard_map.118 = (f32[16,560,128]{2,1,0:T(8,128)}, f32[32,4096]{1,0:T(8,128)S(1)}, f32[32,64]{1,0:T(8,128)S(1)}, f32[8,112,128]{2,1,0:T(8,128)S(1)}, s32[16,8,12...) custom-call(f32[32,4096]{1,0:T(8,128)S(1)} %copy-done.3, f32[3,4096]{1,0:T(4,128)S(1)} %copy-done.6, ...), custom_call_target="tpu_custom_call" | custom-call | tf_op jit(solution)/shard_map/pallas_call | solution.py:566
  58.4 0.0 copy-start.4
  58.4 0.8 copy-done.4
  59.2 0.6 copy-done.7
  59.8 0.6 copy-done.8
  60.4 52.7 %shard_map.119.acc_ref = f32[8,448,128]{2,1,0:T(8,128)} custom-call(f32[16,560,128]{2,1,0:T(8,128)} %get-tuple-element.11.g_ref, f32[8,112,128]{2,1,0:T(8,128)} %copy-done.4, s32[16,8,128]{2,1,0:T(8,128)} %copy-done.7, s32[8,8,128]{2,1,0:T(8,128)} %copy-done.8), custom_call_target="tpu_custom_call" | custom-call | tf_op jit(solution)/shard_map/pallas_call | solution.py:596
  113.1 1.5 %copy-done = f32[8,448,128]{2,1,0:T(8,128)S(1)} copy-done((f32[8,448,128]{2,1,0:T(8,128)S(1)}, f32[8,448,128]{2,1,0:T(8,128)}, u32[]{:S(2)}) %copy-start) | copy-done | bytes 1835032
  114.6 20.4 %shard_map.120 = f32[32,4096]{1,0:T(8,128)S(1)} custom-call(f32[8,448,128]{2,1,0:T(8,128)S(1)} %copy-done, f32[32,64]{1,0:T(8,128)S(1)} %get-tuple-element.15.far_ref, f32[30,64,64]{2,1,0:T(8,128)S(1)} %bitcast.17, f32[16,64,256]{2,1,0:T(8,128)S(1)} %copy-done.1, f32[32,4096]{1,0:T(8,128)S(1)} %get-tuple-element.16.near_ref), custom_call_target="tpu_custom_call" | custom-call | tf_op jit(solution)/shard_map/pallas_call | solution.py:614
  135.0 0.8 copy.18
  (9 shorter events, 0.0 us)
Async XLA Ops:
  2.9 8.3 %copy-start.1 = (f32[16,64,256]{2,1,0:T(8,128)S(1)}, f32[16,64,256]{2,1,0:T(8,128)}, u32[]{:S(2)}) copy-start(f32[16,64,256]{2,1,0:T(8,128)} %base_ref.3) | copy-start | bytes 3145732
  2.9 8.3 %copy-start.2 = (f32[1,30,64,64]{3,2,1,0:T(8,128)S(1)}, f32[1,30,64,64]{3,2,1,0:T(8,128)}, u32[]{:S(2)}) copy-start(f32[1,30,64,64]{3,2,1,0:T(8,128)} %param.15) | copy-start | bytes 1474564
  2.9 8.3 %copy-start.3 = (f32[32,4096]{1,0:T(8,128)S(1)}, f32[32,4096]{1,0:T(8,128)}, u32[]{:S(2)}) copy-start(f32[32,4096]{1,0:T(8,128)} %vec_ref.1) | copy-start | bytes 1572868
  2.9 8.3 %copy-start.5 = (f32[3,16256]{1,0:T(4,128)S(1)}, f32[3,16256]{1,0:T(4,128)}, u32[]{:S(2)}) copy-start(f32[3,16256]{1,0:T(4,128)} %upp_ref.1) | copy-start | bytes 585220
  2.9 8.3 %copy-start.6 = (f32[3,4096]{1,0:T(4,128)S(1)}, f32[3,4096]{1,0:T(4,128)}, u32[]{:S(2)}) copy-start(f32[3,4096]{1,0:T(4,128)} %pts_ref.1) | copy-start | bytes 147460
  3.0 8.3 %copy-start.9 = (f32[3,1792]{1,0:T(4,128)S(1)}, f32[3,1792]{1,0:T(4,128)}, u32[]{:S(2)}) copy-start(f32[3,1792]{1,0:T(4,128)} %skel_ref.1) | copy-start | bytes 64516
  58.4 0.8 copy-start.4
  59.2 0.6 copy-start.7
  59.8 0.6 copy-start.8
  113.1 1.5 %copy-start = (f32[8,448,128]{2,1,0:T(8,128)S(1)}, f32[8,448,128]{2,1,0:T(8,128)}, u32[]{:S(2)}) copy-start(f32[8,448,128]{2,1,0:T(8,128)} %shard_map.119.acc_ref) | copy-start | bytes 5505028

commit v2 on v1

v2 whole, which is shorter than its diff:
```python
import functools
import math

import jax
import jax.numpy as jnp
from jax import lax
from jax.experimental import pallas as pl
from jax.experimental.pallas import tpu as pltpu
from jax.sharding import PartitionSpec as P

F32 = jnp.float32
BF16 = jnp.bfloat16
MESH = pl.DeviceIdType.MESH
LN2 = math.log(2.0)
KAPPA = math.sqrt(3.0) / 0.3 / LN2
TINY = 1e-30

VEC = 32
RANK = 64
LEAF = 256
LEAVES = 16
PTS = 8
LEAFS = 16
PAIRS = 14
NODES = 28
COEF_ROWS = PAIRS * VEC
PAY_ROWS = COEF_ROWS + 48
UPPER = 7
UPN = 254
GROUPS = NODES // 4
DEPTH = 48
NN = (((1,), (0,)), ((), ()))
NT = (((1,), (1,)), ((), ()))


def dg(a, b, dims):
    return lax.dot_general(a, b, dims, preferred_element_type=F32)


def split(x):
    hi = x.astype(BF16)
    return hi, (x - hi.astype(F32)).astype(BF16)


def dot3(a, b, dims):
    ah, al = split(a)
    bh, bl = split(b)
    return dg(ah, bh, dims) + (dg(ah, bl, dims) + dg(al, bh, dims))


def split3(x):
    h = x.astype(BF16).astype(F32)
    r = x - h
    m = r.astype(BF16).astype(F32)
    return h, m, r - m


def scaled(pts):
    return (pts - 0.5) * KAPPA


def forms(x):
    n = x.shape[1]
    x = jnp.concatenate([x, jnp.zeros((5, n), F32)], axis=0)
    q = jnp.sum(x * x, axis=0, keepdims=True)
    row = lax.broadcasted_iota(jnp.int32, (8, n), 0)
    w = jnp.where(row < 3, x, jnp.where(row == 3, 1.0, jnp.where(row == 4, q, 0.0)))
    u = jnp.where(row < 3, -2.0 * x, jnp.where(row == 3, q, jnp.where(row == 4, 1.0, 0.0)))
    return u, w


def stack_u(u):
    h, m, l = split3(u)
    return jnp.concatenate([h, h, m, m, h, l], axis=0)


def stack_w(w):
    h, m, l = split3(w)
    return jnp.concatenate([h, m, h, m, l, h], axis=0)


def matern(squared):
    squared = jnp.maximum(squared, TINY)
    t = squared * lax.rsqrt(squared)
    return (1.0 + LN2 * t) * jnp.exp2(-t)


def pair_matrix(lt_ref, n):
    return jnp.concatenate([lt_ref[2 * n], lt_ref[2 * n + 1]], axis=1)


def up_offset(u):
    return 0 if u == 0 else 256 - (128 >> (u - 1))


def gather_kernel(
    vec_ref, pts_ref, base_ref, lt_ref, skel_ref, upt_ref, upp_ref, sc_ref, tc_ref,
    g_ref, near_ref, far_ref, tp_ref, scg_ref, tcg_ref,
    u_scr, w_scr, v_scr, halo_src, halo_dst, pay, tpay, up_all, ut, xs, xr, sf,
    ssem, rsem, lsem,
):
    leaf = lax.axis_index("leaf")
    p = lax.axis_index("pts")
    me = leaf * PTS + p
    y = leaf // 4
    z = lax.rem(leaf, 4)
    nxt = lax.rem(me + 1, 128)
    prv = lax.rem(me + 127, 128)
    nxt_dev = (nxt // PTS, lax.rem(nxt, PTS))
    prv_dev = (prv // PTS, lax.rem(prv, PTS))

    barrier = pltpu.get_barrier_semaphore()
    for k in range(1, LEAFS):
        pl.semaphore_signal(barrier, inc=1, device_id=(leaf ^ k, p), device_id_type=MESH)
    for k in range(1, PTS):
        pl.semaphore_signal(barrier, inc=1, device_id=(leaf, p ^ k), device_id_type=MESH)
    pl.semaphore_signal(barrier, inc=1, device_id=nxt_dev, device_id_type=MESH)
    pl.semaphore_signal(barrier, inc=1, device_id=prv_dev, device_id_type=MESH)

    counter = [0]
    sends = []

    def remote(src, dst, dev):
        i = counter[0]
        counter[0] += 1
        copy = pltpu.make_async_remote_copy(
            src_ref=src, dst_ref=dst, send_sem=ssem.at[i], recv_sem=rsem.at[i],
            device_id=dev, device_id_type=MESH,
        )
        copy.start()
        sends.append(copy)
        return copy

    locals_ = []

    def local(src, dst):
        copy = pltpu.make_async_copy(src, dst, lsem.at[len(locals_)])
        copy.start()
        locals_.append(copy)

    local(upt_ref, up_all)

    for side, off in ((0, 0), (1, (LEAVES - 1) * LEAF)):
        halo_src[side, 0:VEC] = vec_ref[:, off:off + LEAF]
        halo_src[side, VEC:VEC + 8] = jnp.concatenate(
            [pts_ref[:, off:off + LEAF], jnp.zeros((5, LEAF), F32)], axis=0
        )
    pay[PAY_ROWS - 8:PAY_ROWS] = jnp.zeros((8, 128), F32)
    for a in range(PAIRS):
        x = scaled(skel_ref[:, a * 128:(a + 1) * 128])
        tpay[a * 8:(a + 1) * 8] = forms(x)[0]
        for c in range(3):
            row = COEF_ROWS + c * PAIRS + a
            pay[row:row + 1] = x[c:c + 1]

    lows = (0, LEAVES // 4 * RANK)
    sizes = (LEAVES // 4 * RANK, PAY_ROWS - LEAVES // 4 * RANK)

    def lid(yy, zz):
        return lax.rem(yy + 4, 4) * 4 + lax.rem(zz + 4, 4)

    def near_id(h, stage, step):
        return lid(y, z + step) if (h == 0) == (stage == 0) else lid(y + step, z)

    def block_id(h, first, second):
        return lid(y + second, z + first) if h == 0 else lid(y + first, z + second)

    stage1 = {}
    stage2 = {}

    def begin(h):
        rows = pl.ds(lows[h], sizes[h])
        for step in (1, -1):
            stage1[h, step] = remote(
                pay.at[rows], g_ref.at[leaf, rows], (near_id(h, 0, step), p)
            )

    def spread(h, first):
        rows = pl.ds(lows[h], sizes[h])
        blk = near_id(h, 0, first)
        src = pay.at[rows] if first == 0 else g_ref.at[blk, rows]
        for step in (1, -1):
            stage2[h, first, step] = remote(
                src, g_ref.at[blk, rows], (near_id(h, 1, step), p)
            )

    def forward(h, stage, blk_minus, blk_plus, got_minus, got_plus):
        part = sizes[h] // 16 * 8
        got_minus.wait_recv()
        rows = pl.ds(lows[h], part)
        one = remote(g_ref.at[blk_minus, rows], g_ref.at[blk_minus, rows], (near_id(h, stage, 1), p))
        got_plus.wait_recv()
        rows = pl.ds(lows[h] + part, sizes[h] - part)
        two = remote(g_ref.at[blk_plus, rows], g_ref.at[blk_plus, rows], (near_id(h, stage, -1), p))
        return one, two

    level = [
        dot3(base_ref[n], vec_ref[:, n * LEAF:(n + 1) * LEAF], NT) for n in range(LEAVES)
    ]
    base = 0
    row = 0
    while len(level) > 1:
        if row < COEF_ROWS:
            for g in range(len(level) // 4):
                pay[row:row + RANK] = jnp.concatenate(level[4 * g:4 * g + 4], axis=1)
                row += RANK
        if row == sizes[0]:
            pl.semaphore_wait(barrier, LEAFS + PTS)
            begin(0)
            spread(0, 0)
        if row == COEF_ROWS and len(level) == 4:
            begin(1)
            spread(1, 0)
        level = [
            dot3(
                pair_matrix(lt_ref, base + i),
                jnp.concatenate([level[2 * i], level[2 * i + 1]], axis=0),
                NN,
            )
            for i in range(len(level) // 2)
        ]
        base += len(level)
    root = level[0].T
    xs[0] = root
    upward = {0: remote(xs.at[0], xr.at[0], (leaf, p ^ 1))}

    h0 = remote(halo_src.at[0], halo_dst.at[1], prv_dev)
    h1 = remote(halo_src.at[1], halo_dst.at[0], nxt_dev)
    arrivals = []
    for k in range(1, PTS):
        arrivals.append(remote(tpay, tp_ref.at[p], (leaf, p ^ k)))
        arrivals.append(remote(tc_ref, tcg_ref.at[p], (leaf, p ^ k)))
    for k in range(1, LEAFS):
        arrivals.append(remote(sc_ref, scg_ref.at[leaf], (leaf ^ k, p)))
    local(tpay, tp_ref.at[p])
    local(tc_ref, tcg_ref.at[p])
    local(sc_ref, scg_ref.at[leaf])

    local(pay, g_ref.at[leaf])

    r16 = lax.broadcasted_iota(jnp.int32, (16, UPN), 0)
    c16 = lax.broadcasted_iota(jnp.int32, (16, UPN), 1)
    pick = jnp.zeros((16, UPN), F32)
    for u in range(UPPER):
        first = up_offset(u) + lax.shift_right_logical(me, u + 1) * 2
        pick = jnp.where(jnp.logical_and(r16 // 2 == u, c16 == first + (r16 & 1)), 1.0, pick)
    pick = pick.astype(BF16)
    locals_[0].wait()

    @pl.loop(0, RANK // 2)
    def _(r):
        h, l = split(up_all[pl.ds(pl.multiple_of(r * 128, 128), 128), :])
        got = dg(pick, h, NT) + dg(pick, l, NT)
        ut[pl.ds(2 * r, 16, stride=RANK), :] = got[:, :RANK]
        ut[pl.ds(2 * r + 1, 16, stride=RANK), :] = got[:, RANK:]

    def upper(u, k):
        return ut[(2 * u + k) * RANK:(2 * u + k + 1) * RANK, :]

    opposite = {}

    def step_a():
        for h in range(2):
            opposite[h] = forward(
                h, 0, near_id(h, 0, -1), near_id(h, 0, 1), stage1[h, 1], stage1[h, -1]
            )
            spread(h, -1)
            spread(h, 1)

    def step_b():
        for h in range(2):
            opposite[h][0].wait_recv()
            opposite[h][1].wait_recv()
            spread(h, 2)

    last = []

    def step_c(first):
        for h in range(2):
            last.extend(
                forward(
                    h, 1, block_id(h, first, -1), block_id(h, first, 1),
                    stage2[h, first, 1], stage2[h, first, -1],
                )
            )

    def send_up(u, value):
        xs[u] = value
        dev = (leaf, p ^ (1 << u)) if u < 3 else (leaf ^ (1 << (u - 3)), p)
        upward[u] = remote(xs.at[u], xr.at[u], dev)

    def climb(u):
        upward[u].wait_recv()
        node = lax.shift_right_logical(me, u)
        left_side = lax.rem(node, 2) == 0
        own = xs[u]
        sib = xr[u]
        pair = jnp.concatenate(
            [jnp.where(left_side, own, sib), jnp.where(left_side, sib, own)], axis=1
        )
        if u < UPPER - 1:
            mat = jnp.concatenate([upper(u, 0), upper(u, 1)], axis=1)
            send_up(u + 1, dot3(pair, mat, NT))
        col = pl.multiple_of((up_offset(u) + (node // 2) * 2) * RANK, 128)
        u8, w8 = forms(scaled(upp_ref[:, pl.ds(col, 128)]))
        kern = matern(dg(stack_u(u8).T.astype(BF16), stack_w(w8).astype(BF16), NN))
        lane_left = lax.broadcasted_iota(jnp.int32, (VEC, 2 * RANK), 1) < RANK
        only_sib = jnp.where(jnp.logical_xor(lane_left, left_side), pair, 0.0)
        out = dot3(only_sib, kern, NN)
        sf[u] = jnp.where(left_side, out[:, :RANK], out[:, RANK:])

    def prepare(slot, vec, pts):
        vh, vl = split(vec)
        lanes = pl.ds(pl.multiple_of(slot * LEAF, LEAF), LEAF)
        v_scr[0:VEC, lanes] = vh
        v_scr[VEC:2 * VEC, lanes] = vl
        u8, w8 = forms(scaled(pts))
        w_scr[:, lanes] = stack_w(w8).astype(BF16)
        u_scr[lanes, :] = stack_u(u8).T.astype(BF16)

    @pl.loop(0, LEAVES)
    def _(m):
        lanes = pl.ds(pl.multiple_of(m * LEAF, LEAF), LEAF)
        prepare(m + 1, vec_ref[:, lanes], pts_ref[:, lanes])

    def near(m):
        lanes = pl.ds(pl.multiple_of(m * LEAF, LEAF), LEAF)
        w = w_scr[:, lanes]
        total = None
        for b in range(3):
            src = pl.ds(pl.multiple_of((m - 1 + b) * LEAF, LEAF), LEAF)
            kh, kl = split(matern(dg(u_scr[src, :], w, NN)))
            v = v_scr[:, src]
            big = dg(v, kh, NN)
            part = big[:VEC] + (big[VEC:] + dg(v[:VEC], kl, NN))
            total = part if total is None else total + part
        near_ref[:, pl.ds(pl.multiple_of((m - 1) * LEAF, LEAF), LEAF)] = total

    def near_span(lo, hi):
        @pl.loop(lo, hi)
        def _(m):
            near(m)

    step_a()
    climb(0)
    near_span(2, 3)
    climb(1)
    near_span(3, 4)
    step_b()
    climb(2)
    near_span(4, 6)
    step_c(0)
    climb(3)
    near_span(6, 8)
    climb(4)
    near_span(8, 10)
    step_c(-1)
    climb(5)
    near_span(10, 12)
    step_c(1)
    climb(6)
    near_span(12, 14)
    step_c(2)
    near_span(14, 16)
    h0.wait_recv()
    h1.wait_recv()
    for side, slot, edge in ((0, 0, 0), (1, LEAVES + 1, 127)):
        vec = jnp.where(me == edge, 0.0, halo_dst[side, 0:VEC])
        prepare(slot, vec, halo_dst[side, VEC:VEC + 3])
    near(1)
    near(LEAVES)

    far = sf[UPPER - 1]
    for u in range(UPPER - 2, -1, -1):
        left_side = lax.rem(lax.shift_right_logical(me, u), 2) == 0
        mat = jnp.where(left_side, upper(u, 0), upper(u, 1))
        far = sf[u] + dot3(far, mat, NN)
    far_ref[...] = far

    for c in arrivals:
        c.wait_recv()
    for c in last:
        c.wait_recv()
    for c in sends:
        c.wait_send()
    for c in locals_[1:]:
        c.wait()


def couple_kernel(
    g_hbm, tp_hbm, sc_hbm, tc_hbm, o_ref, g_ref, tp_ref, sc_ref, tc_ref, sem, ct, wt, ut, masks, sums, d_scr, k_scr, acc_a, acc_b,
):
    leaf = lax.axis_index("leaf")
    p = lax.axis_index("pts")
    lane = lax.broadcasted_iota(jnp.int32, (16, 128), 1)
    low = lax.broadcasted_iota(jnp.int32, (RANK, 128), 1) < RANK

    def rows_of(index, size):
        return pl.ds(pl.multiple_of(index * size, size), size)

    blocks = [pltpu.make_async_copy(g_hbm.at[s], g_ref.at[s], sem.at[s]) for s in range(LEAFS)]
    others = [
        pltpu.make_async_copy(a, b, sem.at[LEAFS + i])
        for i, (a, b) in enumerate(((tp_hbm, tp_ref), (sc_hbm, sc_ref), (tc_hbm, tc_ref)))
    ]
    for copy in blocks + others:
        copy.start()

    for q in range(4):
        masks[q] = (lane // VEC == q).astype(F32).astype(BF16)
    for q in range(2):
        masks[4 + q] = (lane // RANK == q).astype(F32).astype(BF16)
    r = lax.broadcasted_iota(jnp.int32, (512, 128), 0)
    c = lax.broadcasted_iota(jnp.int32, (512, 128), 1)
    sums[...] = jnp.logical_and(
        lax.rem(r, VEC) == lax.rem(c, VEC), r // 128 == c // VEC
    ).astype(F32).astype(BF16)

    def masked(x, m):
        return (x.reshape(-1, 16, 128) * masks[m][None]).reshape(x.shape)

    @pl.loop(0, LEAFS)
    def _(s):
        pltpu.make_async_copy(g_hbm.at[s], g_ref.at[s], sem.at[s]).wait()
        for g in range(GROUPS):
            c = g_ref[s, g * RANK:(g + 1) * RANK, :]
            for j in range(2):
                h, l = split(pltpu.roll(c, RANK, 1) if j else c)
                rows = (s * GROUPS + g) * 2 + j
                ct[rows_of(rows, 2 * RANK), :] = jnp.concatenate([h, l], axis=0)
        for a in range(PAIRS):
            x = jnp.concatenate(
                [
                    g_ref[s, COEF_ROWS + c * PAIRS + a:COEF_ROWS + c * PAIRS + a + 1, :]
                    for c in range(3)
                ],
                axis=0,
            )
            w = forms(x)[1]
            for j in range(2):
                rows = (s * PAIRS + a) * 2 + j
                wt[rows_of(rows, DEPTH), :] = stack_w(
                    pltpu.roll(w, RANK, 1) if j else w
                ).astype(BF16)

    for copy in others:
        copy.wait()
    ut[NODES * RANK:(NODES + 1) * RANK, :] = jnp.zeros((RANK, 2 * DEPTH), BF16)
    slot_a = lax.broadcasted_iota(jnp.int32, (RANK, 2 * DEPTH), 1) < DEPTH

    @pl.loop(0, PTS)
    def _(d):
        for a in range(PAIRS):
            t = stack_u(tp_ref[d, a * 8:(a + 1) * 8, :])
            ut[2 * a * RANK:(2 * a + 2) * RANK, :] = jnp.concatenate([t, t], axis=0).T.astype(BF16)
        acc_a[...] = jnp.zeros_like(acc_a)
        acc_b[...] = jnp.zeros_like(acc_b)

        @pl.loop(0, 3)
        def _(lev):
            ids = []
            for s in range(LEAFS):
                na = s * NODES + sc_ref[s, lev * 2, leaf * PTS + d]
                nb = s * NODES + sc_ref[s, lev * 2 + 1, leaf * PTS + d]
                ra = rows_of(tc_ref[d, lev * 2, s * PTS + p], RANK)
                rb = rows_of(tc_ref[d, lev * 2 + 1, s * PTS + p], RANK)
                ids.append((na, nb, ra, rb))
            for s, (na, nb, ra, rb) in enumerate(ids):
                u = jnp.where(slot_a, ut[ra, :], ut[rb, :])
                wa = masked(wt[rows_of(na, DEPTH), :], 4)
                wb = masked(wt[rows_of(nb ^ 1, DEPTH), :], 5)
                d_scr[s * RANK:(s + 1) * RANK] = dg(u, jnp.concatenate([wa, wb], axis=0), NN)
            for s in range(LEAFS):
                h, l = split(matern(d_scr[s * RANK:(s + 1) * RANK]))
                k_scr[s * RANK:(s + 1) * RANK] = jnp.concatenate([h, l, h], axis=1)
            for s, (na, nb, ra, rb) in enumerate(ids):
                xa = masked(ct[rows_of(na >> 1, 2 * RANK), :], na & 1)
                xb = masked(ct[rows_of((nb >> 1) ^ 1, 2 * RANK), :], 2 + (nb & 1))
                high = jnp.concatenate([xa[:RANK], xb[:RANK]], axis=0)
                rest = jnp.concatenate([xa[RANK:], xb[RANK:]], axis=0)
                k = k_scr[s * RANK:(s + 1) * RANK]
                part = dg(k, jnp.concatenate([high, high, rest], axis=0), NN)
                acc_a[ra, :] += part
                acc_b[rb, :] += part

        for g in range(GROUPS):
            parts = []
            for q in range(4):
                rows = slice((4 * g + q) * RANK, (4 * g + q + 1) * RANK)
                parts.append(jnp.where(low, acc_a[rows, :], acc_b[rows, :]))
            h, l = split(jnp.concatenate(parts, axis=1))
            o_ref[d, g * RANK:(g + 1) * RANK, :] = dg(h, sums[...], NN) + dg(l, sums[...], NN)


def scatter_kernel(
    acc_hbm, far_hbm, lt_hbm, base_hbm, near_hbm, out_ref,
    acc_ref, far_ref, lt_ref, base_ref, near_ref, from_core, s1, s2, work, ssem, rsem, lsem,
):
    leaf = lax.axis_index("leaf")
    p = lax.axis_index("pts")
    x = p // 2
    core = lax.rem(p, 2)
    sister = (leaf, p ^ 1)

    own_blocks = {}
    steps = (2, 1, 3, 0)
    for st in steps:
        blk = lax.rem(x + st, 4) * 2 + core
        own_blocks[st] = pltpu.make_async_copy(acc_hbm.at[blk], acc_ref.at[st], lsem.at[st])
        own_blocks[st].start()
    others = [
        pltpu.make_async_copy(a, b, lsem.at[4 + i])
        for i, (a, b) in enumerate(
            ((far_hbm, far_ref), (lt_hbm, lt_ref), (base_hbm, base_ref), (near_hbm, near_ref))
        )
    ]
    for copy in others:
        copy.start()

    def dev(step):
        return (leaf, lax.rem(x + step + 4, 4) * 2 + core)

    barrier = pltpu.get_barrier_semaphore()
    for d in (sister, dev(1), dev(-1)):
        pl.semaphore_signal(barrier, inc=1, device_id=d, device_id_type=MESH)
    pl.semaphore_wait(barrier, 3)

    sends = []

    def remote(src, dst, device):
        i = len(sends)
        copy = pltpu.make_async_remote_copy(
            src_ref=src, dst_ref=dst, send_sem=ssem.at[i], recv_sem=rsem.at[i],
            device_id=device, device_id_type=MESH,
        )
        copy.start()
        sends.append(copy)
        return copy

    half = COEF_ROWS // 2
    first = {}
    for st in steps:
        xx = lax.rem(x + st, 4)
        first[st] = remote(acc_hbm.at[xx * 2 + 1 - core], from_core.at[st], sister)

    def summed(st):
        first[st].wait_recv()
        own_blocks[st].wait()
        return acc_ref[st] + from_core[st]

    work[0] = summed(2)
    a1 = remote(work.at[0, pl.ds(0, half)], s1.at[pl.ds(0, half)], dev(1))
    b1 = remote(work.at[0, pl.ds(half, half)], s1.at[pl.ds(half, half)], dev(-1))
    work[1] = summed(1)
    work[2] = summed(3)
    a1.wait_recv()
    work[1, 0:half] += s1[0:half]
    a2 = remote(work.at[1], s2.at[0], dev(1))
    b1.wait_recv()
    work[2, half:] += s1[half:]
    b2 = remote(work.at[2], s2.at[1], dev(-1))

    def down(node, n):
        return dot3(node, pair_matrix(lt_ref, n), NN)

    for copy in others:
        copy.wait()
    top = down(far_ref[...], 14)
    level2 = [down(top[:, :RANK], 12), down(top[:, RANK:], 13)]
    own = summed(0)
    a2.wait_recv()
    b2.wait_recv()
    work[3] = own + (s2[0] + s2[1])

    turned = [work[3, g * RANK:(g + 1) * RANK].T for g in range(GROUPS)]

    def coupling(a):
        t = turned[a // 2]
        r = (a % 2) * 2 * VEC
        return jnp.concatenate([t[r:r + VEC], t[r + VEC:r + 2 * VEC]], axis=1)

    pairs = [level2[i] + coupling(12 + i) for i in range(2)]
    pairs = [
        down(pairs[i // 2][:, (i % 2) * RANK:(i % 2 + 1) * RANK], 8 + i) + coupling(8 + i)
        for i in range(4)
    ]
    pairs = [
        down(pairs[i // 2][:, (i % 2) * RANK:(i % 2 + 1) * RANK], i) + coupling(i)
        for i in range(8)
    ]
    for m in range(LEAVES):
        c = pairs[m // 2][:, (m % 2) * RANK:(m % 2 + 1) * RANK]
        cols = slice(m * LEAF, (m + 1) * LEAF)
        out_ref[:, cols] = near_ref[:, cols] + dot3(c, base_ref[m], NN)
    for c in sends:
        c.wait_send()


def vmem():
    return pl.BlockSpec(memory_space=pltpu.VMEM)


def anywhere():
    return pl.BlockSpec(memory_space=pl.ANY)


def shape(*dims, dtype=F32):
    return jax.ShapeDtypeStruct(dims, dtype)


def on_device(
    vectors, points, leaf_bases, local_transfer, skel_points, up_transfer, up_points,
    source_ids, target_ids, live_counts,
):
    me = lax.axis_index("leaf") * PTS + lax.axis_index("pts")
    counts = jnp.array([LEAVES, LEAVES // 2, LEAVES // 4], jnp.int32)
    starts = jnp.array([0, LEAVES, LEAVES + LEAVES // 2], jnp.int32)
    shift = (starts - me * counts)[:, None, None]
    slot = jnp.arange(2, dtype=jnp.int32)
    source_code = jnp.swapaxes(source_ids[:, 0], 1, 2) + shift
    target_code = jnp.where(
        slot[None, :, None] < live_counts[:, 0, None, :],
        jnp.swapaxes(target_ids[:, 0], 1, 2) + shift,
        NODES,
    )
    source_code = jnp.pad(source_code.reshape(6, 128), ((0, 2), (0, 0)))
    target_code = jnp.pad(target_code.reshape(6, 128), ((0, 2), (0, 0)))
    lt = local_transfer[0]
    up_rows = jnp.transpose(up_transfer, (1, 2, 0)).reshape(RANK * RANK, UPN)
    n_remote = 96

    gathered, near, far, tp, scg, tcg = pl.pallas_call(
        gather_kernel,
        out_shape=(
            shape(LEAFS, PAY_ROWS, 128), shape(VEC, LEAVES * LEAF), shape(VEC, RANK),
            shape(PTS, PAIRS * 8, 128), shape(LEAFS, 8, 128, dtype=jnp.int32),
            shape(PTS, 8, 128, dtype=jnp.int32),
        ),
        in_specs=[vmem()] * 5 + [anywhere()] + [vmem()] * 3,
        out_specs=(vmem(),) * 6,
        scratch_shapes=[
            pltpu.VMEM((18 * LEAF, DEPTH), BF16),
            pltpu.VMEM((DEPTH, 18 * LEAF), BF16),
            pltpu.VMEM((2 * VEC, 18 * LEAF), BF16),
            pltpu.VMEM((2, VEC + 8, LEAF), F32),
            pltpu.VMEM((2, VEC + 8, LEAF), F32),
            pltpu.VMEM((PAY_ROWS, 128), F32),
            pltpu.VMEM((PAIRS * 8, 128), F32),
            pltpu.VMEM((RANK * RANK, UPN), F32),
            pltpu.VMEM((16 * RANK, RANK), F32),
            pltpu.VMEM((UPPER, VEC, RANK), F32),
            pltpu.VMEM((UPPER, VEC, RANK), F32),
            pltpu.VMEM((UPPER, VEC, RANK), F32),
            pltpu.SemaphoreType.DMA((n_remote,)),
            pltpu.SemaphoreType.DMA((n_remote,)),
            pltpu.SemaphoreType.DMA((16,)),
        ],
        compiler_params=pltpu.CompilerParams(
            collective_id=0, has_side_effects=True, vmem_limit_bytes=48 << 20
        ),
    )(vectors, points, leaf_bases, lt, skel_points, up_rows, up_points, source_code, target_code)

    partial = pl.pallas_call(
        couple_kernel,
        out_shape=shape(PTS, COEF_ROWS, 128),
        in_specs=[anywhere()] * 4,
        out_specs=vmem(),
        scratch_shapes=[
            pltpu.VMEM((LEAFS, PAY_ROWS, 128), F32),
            pltpu.VMEM((PTS, PAIRS * 8, 128), F32),
            pltpu.SMEM((LEAFS, 8, 128), jnp.int32),
            pltpu.SMEM((PTS, 8, 128), jnp.int32),
            pltpu.SemaphoreType.DMA((LEAFS + 3,)),
            pltpu.VMEM((LEAFS * GROUPS * 4 * RANK, 128), BF16),
            pltpu.VMEM((LEAFS * NODES * DEPTH, 128), BF16),
            pltpu.VMEM(((NODES + 1) * RANK, 2 * DEPTH), BF16),
            pltpu.VMEM((8, 16, 128), BF16),
            pltpu.VMEM((512, 128), BF16),
            pltpu.VMEM((LEAFS * RANK, 128), F32),
            pltpu.VMEM((LEAFS * RANK, 3 * 128), BF16),
            pltpu.VMEM(((NODES + 1) * RANK, 128), F32),
            pltpu.VMEM(((NODES + 1) * RANK, 128), F32),
        ],
        compiler_params=pltpu.CompilerParams(vmem_limit_bytes=56 << 20),
    )(gathered, tp, scg, tcg)

    return pl.pallas_call(
        scatter_kernel,
        out_shape=shape(VEC, LEAVES * LEAF),
        in_specs=[anywhere()] * 5,
        out_specs=vmem(),
        scratch_shapes=[
            pltpu.VMEM((4, COEF_ROWS, 128), F32),
            pltpu.VMEM((VEC, RANK), F32),
            pltpu.VMEM((30, RANK, RANK), F32),
            pltpu.VMEM((LEAVES, RANK, LEAF), F32),
            pltpu.VMEM((VEC, LEAVES * LEAF), F32),
            pltpu.VMEM((4, COEF_ROWS, 128), F32),
            pltpu.VMEM((COEF_ROWS, 128), F32),
            pltpu.VMEM((2, COEF_ROWS, 128), F32),
            pltpu.VMEM((4, COEF_ROWS, 128), F32),
            pltpu.SemaphoreType.DMA((8,)),
            pltpu.SemaphoreType.DMA((8,)),
            pltpu.SemaphoreType.DMA((8,)),
        ],
        compiler_params=pltpu.CompilerParams(
            collective_id=1, has_side_effects=True, vmem_limit_bytes=48 << 20
        ),
    )(partial, far, lt, leaf_bases, near)


def solution(mesh):
    both = ("leaf", "pts")
    return jax.shard_map(
        on_device,
        mesh=mesh,
        in_specs=(
            P(None, both),
            P(None, both),
            P(both, None, None),
            P(both, None, None, None),
            P(None, both),
            P(),
            P(),
            P(None, both, None, None),
            P(None, both, None, None),
            P(None, both, None),
        ),
        out_specs=P(None, both),
        check_vma=False,
    )
```

time: 136 us -> 115 us (0.85)
  Pallas kernels: 120 us -> 101 us
  local copies, waits for them, and re-layouts: 13.3 us -> 11 us
    pallas_call x1, Pallas kernels: 52.7 us -> 29.5 us  [on_device(): pl.pallas_call(couple_kernel, out_shape=shape(PTS, COEF_ROWS, 128), in_sp...]
    unnamed x23 -> x26, local copies, waits for them, and re-layouts: 13.2 us -> 11 us
    pallas_call x1, Pallas kernels: 20.4 us -> 22.5 us  [on_device(): pl.pallas_call(scatter_kernel, out_shape=shape(VEC, LEAVES * LEAF), in_sp...]
    pallas_call x1, Pallas kernels: 47.1 us -> 48.9 us  [on_device(): pl.pallas_call(gather_kernel, out_shape=(shape(LEAFS, PAY_ROWS, 128), sha...]
where the time goes in v2:
time: 115 us; the launch traced here: 114 us
  Pallas kernels  101 us (88%)
  local copies, waits for them, and re-layouts  11 us (10%)
  other arithmetic  2.18 us (2%)
    pallas_call x1, Pallas kernels, on_device(): pl.pallas_call(gather_kernel, out_shape=(shape(LEAFS, PAY_ROWS, 128), sha...  48.9 us
    pallas_call x1, Pallas kernels, on_device(): pl.pallas_call(couple_kernel, out_shape=shape(PTS, COEF_ROWS, 128), in_sp...  29.5 us
    pallas_call x1, Pallas kernels, on_device(): pl.pallas_call(scatter_kernel, out_shape=shape(VEC, LEAVES * LEAF), in_sp...  22.5 us
    unnamed x26, local copies, waits for them, and re-layouts  11 us

profile of v2, /device:TPU:1, one launch (start us, length us, event | category | flops | bytes accessed | tf_op | source)
XLA Modules:
  0.0 114.2 jit_solution(7556063612669017159)
XLA Ops:
  0.0 0.7 multiply_subtract_fusion
  0.7 0.7 copy.15
  1.4 0.8 compare_select_fusion
  2.1 0.8 fusion
  2.9 0.0 copy-start.1
  2.9 1.2 %copy-done.1 = f32[16,64,256]{2,1,0:T(8,128)S(1)} copy-done((f32[16,64,256]{2,1,0:T(8,128)S(1)}, f32[16,64,256]{2,1,0:T(8,128)}, u32[]{:S(2)}) %copy-start.1) | copy-done | bytes 1048600
  4.1 0.0 copy-start.3
  4.1 1.2 %copy-done.3 = f32[1,30,64,64]{3,2,1,0:T(8,128)S(1)} copy-done((f32[1,30,64,64]{3,2,1,0:T(8,128)S(1)}, f32[1,30,64,64]{3,2,1,0:T(8,128)}, u32[]{:S(2)}) %copy-start.3) | copy-done | bytes 491544
  5.3 1.0 copy-done.5
  6.4 0.9 copy-done.7
  7.3 0.8 copy-done.8
  8.2 0.7 copy-done.11
  8.9 48.9 %shard_map.118 = (f32[16,496,128]{2,1,0:T(8,128)}, f32[32,4096]{1,0:T(8,128)S(1)}, f32[32,64]{1,0:T(8,128)S(1)}, f32[8,112,128]{2,1,0:T(8,128)S(1)}, s32[16,8,12...) custom-call(f32[32,4096]{1,0:T(8,128)S(1)} %copy-done.5, f32[3,4096]{1,0:T(4,128)S(1)} %copy-done.8, ...), custom_call_target="tpu_custom_call" | custom-call | tf_op jit(solution)/shard_map/pallas_call | solution.py:632
  57.8 0.0 copy-start.6
  57.8 0.8 copy-done.6
  58.6 0.6 copy-done.9
  59.2 0.6 copy-done.10
  59.8 29.5 %shard_map.119.acc_hbm = f32[8,448,128]{2,1,0:T(8,128)} custom-call(f32[16,496,128]{2,1,0:T(8,128)} %get-tuple-element.11.g_hbm, f32[8,112,128]{2,1,0:T(8,128)} %copy-done.6, s32[16,8,128]{2,1,0:T(8,128)} %copy-done.9, s32[8,8,128]{2,1,0:T(8,128)} %copy-done.10), custom_call_target="tpu_custom_call" | custom-call | tf_op jit(solution)/shard_map/pallas_call | solution.py:663
  89.4 0.0 copy-done.2
  89.4 0.0 copy-done.4
  89.4 0.0 copy-start
  89.4 1.5 %copy-done = f32[8,448,128]{2,1,0:T(8,128)S(1)} copy-done((f32[8,448,128]{2,1,0:T(8,128)S(1)}, f32[8,448,128]{2,1,0:T(8,128)}, u32[]{:S(2)}) %copy-start) | copy-done | bytes 1835032
  90.9 22.5 %shard_map.120 = f32[32,4096]{1,0:T(8,128)S(1)} custom-call(f32[8,448,128]{2,1,0:T(8,128)S(1)} %copy-done, f32[32,64]{1,0:T(8,128)S(1)} %get-tuple-element.15.far_hbm, f32[30,64,64]{2,1,0:T(8,128)S(1)} %bitcast.20, f32[16,64,256]{2,1,0:T(8,128)S(1)} %copy-done.2, f32[32,4096]{1,0:T(8,128)S(1)} %get-tuple-element.16.near_hbm), custom_call_target="tpu_custom_call" | custom-call | tf_op jit(solution)/shard_map/pallas_call | solution.py:687
  113.4 0.8 copy.17
  (12 shorter events, 0.0 us)
Async XLA Ops:
  2.9 1.2 %copy-start.1 = (f32[16,64,256]{2,1,0:T(8,128)S(1)}, f32[16,64,256]{2,1,0:T(8,128)}, u32[]{:S(2)}) copy-start(f32[16,64,256]{2,1,0:T(8,128)} %base_hbm.1) | copy-start | bytes 3145732
  4.1 1.2 %copy-start.3 = (f32[1,30,64,64]{3,2,1,0:T(8,128)S(1)}, f32[1,30,64,64]{3,2,1,0:T(8,128)}, u32[]{:S(2)}) copy-start(f32[1,30,64,64]{3,2,1,0:T(8,128)} %param.15) | copy-start | bytes 1474564
  5.3 1.0 copy-start.5
  6.4 0.9 copy-start.7
  7.3 0.8 copy-start.8
  8.2 0.7 copy-start.11
  57.8 0.8 copy-start.6
  58.6 0.6 copy-start.9
  59.2 0.6 copy-start.10
  59.8 29.5 %copy-start.2 = (f32[16,64,256]{2,1,0:T(8,128)S(1)}, f32[16,64,256]{2,1,0:T(8,128)}, u32[]{:S(2)}) copy-start(f32[16,64,256]{2,1,0:T(8,128)} %base_hbm.1) | copy-start | bytes 3145732
  59.8 29.5 %copy-start.4 = (f32[1,30,64,64]{3,2,1,0:T(8,128)S(1)}, f32[1,30,64,64]{3,2,1,0:T(8,128)}, u32[]{:S(2)}) copy-start(f32[1,30,64,64]{3,2,1,0:T(8,128)} %param.15) | copy-start | bytes 1474564
  89.4 1.5 %copy-start = (f32[8,448,128]{2,1,0:T(8,128)S(1)}, f32[8,448,128]{2,1,0:T(8,128)}, u32[]{:S(2)}) copy-start(f32[8,448,128]{2,1,0:T(8,128)} %shard_map.119.acc_hbm) | copy-start | bytes 5505028

commit v3 on v2

--- a/solution.py
+++ b/solution.py
@@ -27,6 +27,7 @@
 PAY_ROWS = COEF_ROWS + 48
 UPPER = 7
 UPN = 254
+TREE = (0, 8, 12, 14, 30, 38, 42, 44)
 GROUPS = NODES // 4
 DEPTH = 48
 NN = (((1,), (0,)), ((), ()))
@@ -94,9 +95,9 @@
 
 
 def gather_kernel(
-    vec_ref, pts_ref, base_ref, lt_ref, skel_ref, upt_ref, upp_ref, sc_ref, tc_ref,
+    vec_hbm, pts_hbm, base_hbm, lt_hbm, skel_hbm, upt_ref, upp_hbm, src_ref, tgt_ref, live_ref,
     g_ref, near_ref, far_ref, tp_ref, scg_ref, tcg_ref,
-    u_scr, w_scr, v_scr, halo_src, halo_dst, pay, tpay, up_all, ut, xs, xr, sf,
+    vec_ref, pts_ref, base_ref, lt_ref, skel_ref, upp_ref, sc_ref, tc_ref, u_scr, w_scr, v_scr, halo_src, halo_dst, pay, tpay, up_all, ut, tree, sf,
     ssem, rsem, lsem,
 ):
     leaf = lax.axis_index("leaf")
@@ -138,13 +139,22 @@
         copy.start()
         locals_.append(copy)
 
-    local(upt_ref, up_all)
-
-    for side, off in ((0, 0), (1, (LEAVES - 1) * LEAF)):
-        halo_src[side, 0:VEC] = vec_ref[:, off:off + LEAF]
-        halo_src[side, VEC:VEC + 8] = jnp.concatenate(
-            [pts_ref[:, off:off + LEAF], jnp.zeros((5, LEAF), F32)], axis=0
-        )
+    for src, dst in (
+        (skel_hbm, skel_ref), (vec_hbm, vec_ref), (base_hbm, base_ref), (lt_hbm, lt_ref),
+        (pts_hbm, pts_ref), (upp_hbm, upp_ref), (upt_ref, up_all),
+    ):
+        local(src, dst)
+
+    sc_ref[...] = jnp.zeros_like(sc_ref)
+    tc_ref[...] = jnp.zeros_like(tc_ref)
+    for lev in range(3):
+        shift = LEAVES * 2 - (LEAVES * 2 >> lev) - me * (LEAVES >> lev)
+        for k in range(2):
+            row = slice(2 * lev + k, 2 * lev + k + 1)
+            sc_ref[row] = src_ref[lev, k:k + 1] + shift
+            tc_ref[row] = jnp.where(k < live_ref[lev], tgt_ref[lev, k:k + 1] + shift, NODES)
+
+    locals_[0].wait()
     pay[PAY_ROWS - 8:PAY_ROWS] = jnp.zeros((8, 128), F32)
     for a in range(PAIRS):
         x = scaled(skel_ref[:, a * 128:(a + 1) * 128])
@@ -194,6 +204,8 @@
         two = remote(g_ref.at[blk_plus, rows], g_ref.at[blk_plus, rows], (near_id(h, stage, -1), p))
         return one, two
 
+    for i in (1, 2, 3):
+        locals_[i].wait()
     level = [
         dot3(base_ref[n], vec_ref[:, n * LEAF:(n + 1) * LEAF], NT) for n in range(LEAVES)
     ]
@@ -221,9 +233,16 @@
         ]
         base += len(level)
     root = level[0].T
-    xs[0] = root
-    upward = {0: remote(xs.at[0], xr.at[0], (leaf, p ^ 1))}
-
+    tree[p] = root
+    roots = [remote(tree.at[p], tree.at[p], (leaf, p ^ k)) for k in range(1, PTS)]
+
+    for i in (4, 5):
+        locals_[i].wait()
+    for side, off in ((0, 0), (1, (LEAVES - 1) * LEAF)):
+        halo_src[side, 0:VEC] = vec_ref[:, off:off + LEAF]
+        halo_src[side, VEC:VEC + 8] = jnp.concatenate(
+            [pts_ref[:, off:off + LEAF], jnp.zeros((5, LEAF), F32)], axis=0
+        )
     h0 = remote(halo_src.at[0], halo_dst.at[1], prv_dev)
     h1 = remote(halo_src.at[1], halo_dst.at[0], nxt_dev)
     arrivals = []
@@ -238,24 +257,25 @@
 
     local(pay, g_ref.at[leaf])
 
-    r16 = lax.broadcasted_iota(jnp.int32, (16, UPN), 0)
-    c16 = lax.broadcasted_iota(jnp.int32, (16, UPN), 1)
-    pick = jnp.zeros((16, UPN), F32)
-    for u in range(UPPER):
-        first = up_offset(u) + lax.shift_right_logical(me, u + 1) * 2
-        pick = jnp.where(jnp.logical_and(r16 // 2 == u, c16 == first + (r16 & 1)), 1.0, pick)
-    pick = pick.astype(BF16)
-    locals_[0].wait()
-
-    @pl.loop(0, RANK // 2)
-    def _(r):
-        h, l = split(up_all[pl.ds(pl.multiple_of(r * 128, 128), 128), :])
-        got = dg(pick, h, NT) + dg(pick, l, NT)
-        ut[pl.ds(2 * r, 16, stride=RANK), :] = got[:, :RANK]
-        ut[pl.ds(2 * r + 1, 16, stride=RANK), :] = got[:, RANK:]
-
-    def upper(u, k):
-        return ut[(2 * u + k) * RANK:(2 * u + k + 1) * RANK, :]
+    r48 = lax.broadcasted_iota(jnp.int32, (48, UPN), 0)
+    c48 = lax.broadcasted_iota(jnp.int32, (48, UPN), 1)
+    want = jnp.where(
+        r48 < 8, leaf * 8 + r48,
+        jnp.where(r48 < 12, 120 + leaf * 4 + r48, jnp.where(r48 < 14, 180 + leaf * 2 + r48, 210 + r48)),
+    )
+    pick = (c48 == want).astype(F32).astype(BF16)
+
+    def pick_rows(lo, hi):
+        @pl.loop(lo, hi)
+        def _(r):
+            halves = [
+                split(up_all[pl.ds(pl.multiple_of(r * 512 + i * 128, 128), 128), :])
+                for i in range(4)
+            ]
+            got = [dg(pick, h, NT) + dg(pick, l, NT) for h, l in halves]
+            for i, x in enumerate(got):
+                ut[pl.ds(8 * r + 2 * i, 48, stride=RANK), :] = x[:, :RANK]
+                ut[pl.ds(8 * r + 2 * i + 1, 48, stride=RANK), :] = x[:, RANK:]
 
     opposite = {}
 
@@ -284,30 +304,55 @@
                 )
             )
 
-    def send_up(u, value):
-        xs[u] = value
-        dev = (leaf, p ^ (1 << u)) if u < 3 else (leaf ^ (1 << (u - 3)), p)
-        upward[u] = remote(xs.at[u], xr.at[u], dev)
-
-    def climb(u):
-        upward[u].wait_recv()
-        node = lax.shift_right_logical(me, u)
-        left_side = lax.rem(node, 2) == 0
-        own = xs[u]
-        sib = xr[u]
-        pair = jnp.concatenate(
-            [jnp.where(left_side, own, sib), jnp.where(left_side, sib, own)], axis=1
+    def matrix(n):
+        return ut[pl.ds(pl.multiple_of(n * RANK, RANK), RANK), :]
+
+    def parent(n):
+        return dot3(
+            jnp.concatenate([tree[n], tree[n + 1]], axis=1),
+            jnp.concatenate([matrix(n), matrix(n + 1)], axis=1),
+            NT,
         )
-        if u < UPPER - 1:
-            mat = jnp.concatenate([upper(u, 0), upper(u, 1)], axis=1)
-            send_up(u + 1, dot3(pair, mat, NT))
-        col = pl.multiple_of((up_offset(u) + (node // 2) * 2) * RANK, 128)
-        u8, w8 = forms(scaled(upp_ref[:, pl.ds(col, 128)]))
-        kern = matern(dg(stack_u(u8).T.astype(BF16), stack_w(w8).astype(BF16), NN))
+
+    def raise_level(u):
+        return [parent(TREE[u] + 2 * i) for i in range((TREE[u + 1] - TREE[u]) // 2)]
+
+    def own_node(u):
+        return p >> u if u < 3 else leaf >> (u - 3)
+
+    def lower_levels():
+        for c in roots:
+            c.wait_recv()
+        for u in range(2):
+            for i, x in enumerate(raise_level(u)):
+                tree[TREE[u + 1] + i] = x
+        mine = TREE[3] + leaf
+        tree[mine] = raise_level(2)[0]
+        return [remote(tree.at[mine], tree.at[mine], (leaf ^ k, p)) for k in range(1, LEAFS)]
+
+    def upper_levels(tops):
+        for c in tops:
+            c.wait_recv()
+        for u in range(3, 6):
+            for i, x in enumerate(raise_level(u)):
+                tree[TREE[u + 1] + i] = x
+
+    def sibling_fields():
         lane_left = lax.broadcasted_iota(jnp.int32, (VEC, 2 * RANK), 1) < RANK
-        only_sib = jnp.where(jnp.logical_xor(lane_left, left_side), pair, 0.0)
-        out = dot3(only_sib, kern, NN)
-        sf[u] = jnp.where(left_side, out[:, :RANK], out[:, RANK:])
+        distances = []
+        for u in range(UPPER):
+            first = lax.shift_right_logical(me, u + 1) * 2
+            col = pl.multiple_of((up_offset(u) + first) * RANK, 128)
+            u8, w8 = forms(scaled(upp_ref[:, pl.ds(col, 128)]))
+            distances.append(dg(stack_u(u8).T.astype(BF16), stack_w(w8).astype(BF16), NN))
+        kernels = [matern(x) for x in distances]
+        for u in range(UPPER):
+            left_side = lax.rem(own_node(u), 2) == 0
+            sib = tree[TREE[u] + (own_node(u) ^ 1)]
+            pair = jnp.concatenate([sib, sib], axis=1)
+            only_sib = jnp.where(jnp.logical_xor(lane_left, left_side), pair, 0.0)
+            out = dot3(only_sib, kernels[u], NN)
+            sf[u] = jnp.where(left_side, out[:, :RANK], out[:, RANK:])
 
     def prepare(slot, vec, pts):
         vh, vl = split(vec)
@@ -317,11 +362,6 @@
         u8, w8 = forms(scaled(pts))
         w_scr[:, lanes] = stack_w(w8).astype(BF16)
         u_scr[lanes, :] = stack_u(u8).T.astype(BF16)
-
-    @pl.loop(0, LEAVES)
-    def _(m):
-        lanes = pl.ds(pl.multiple_of(m * LEAF, LEAF), LEAF)
-        prepare(m + 1, vec_ref[:, lanes], pts_ref[:, lanes])
 
     def near(m):
         lanes = pl.ds(pl.multiple_of(m * LEAF, LEAF), LEAF)
@@ -342,26 +382,27 @@
             near(m)
 
     step_a()
-    climb(0)
-    near_span(2, 3)
-    climb(1)
-    near_span(3, 4)
+    locals_[6].wait()
+    pick_rows(0, 4)
     step_b()
-    climb(2)
-    near_span(4, 6)
+    pick_rows(4, 8)
+    tops = lower_levels()
     step_c(0)
-    climb(3)
-    near_span(6, 8)
-    climb(4)
-    near_span(8, 10)
+
+    @pl.loop(0, LEAVES)
+    def _(m):
+        lanes = pl.ds(pl.multiple_of(m * LEAF, LEAF), LEAF)
+        prepare(m + 1, vec_ref[:, lanes], pts_ref[:, lanes])
+
+    near_span(2, 6)
     step_c(-1)
-    climb(5)
+    near_span(6, 10)
+    step_c(1)
     near_span(10, 12)
-    step_c(1)
-    climb(6)
-    near_span(12, 14)
+    upper_levels(tops)
     step_c(2)
-    near_span(14, 16)
+    near_span(12, 16)
+    sibling_fields()
     h0.wait_recv()
     h1.wait_recv()
     for side, slot, edge in ((0, 0, 0), (1, LEAVES + 1, 127)):
@@ -372,9 +413,7 @@
 
     far = sf[UPPER - 1]
     for u in range(UPPER - 2, -1, -1):
-        left_side = lax.rem(lax.shift_right_logical(me, u), 2) == 0
-        mat = jnp.where(left_side, upper(u, 0), upper(u, 1))
-        far = sf[u] + dot3(far, mat, NN)
+        far = sf[u] + dot3(far, matrix(TREE[u] + own_node(u)), NN)
     far_ref[...] = far
 
     for c in arrivals:
@@ -383,7 +422,7 @@
         c.wait_recv()
     for c in sends:
         c.wait_send()
-    for c in locals_[1:]:
+    for c in locals_[7:]:
         c.wait()
 
 
@@ -612,22 +651,11 @@
     vectors, points, leaf_bases, local_transfer, skel_points, up_transfer, up_points,
     source_ids, target_ids, live_counts,
 ):
-    me = lax.axis_index("leaf") * PTS + lax.axis_index("pts")
-    counts = jnp.array([LEAVES, LEAVES // 2, LEAVES // 4], jnp.int32)
-    starts = jnp.array([0, LEAVES, LEAVES + LEAVES // 2], jnp.int32)
-    shift = (starts - me * counts)[:, None, None]
-    slot = jnp.arange(2, dtype=jnp.int32)
-    source_code = jnp.swapaxes(source_ids[:, 0], 1, 2) + shift
-    target_code = jnp.where(
-        slot[None, :, None] < live_counts[:, 0, None, :],
-        jnp.swapaxes(target_ids[:, 0], 1, 2) + shift,
-        NODES,
-    )
-    source_code = jnp.pad(source_code.reshape(6, 128), ((0, 2), (0, 0)))
-    target_code = jnp.pad(target_code.reshape(6, 128), ((0, 2), (0, 0)))
+    sources = jnp.swapaxes(source_ids[:, 0], 1, 2)
+    targets = jnp.swapaxes(target_ids[:, 0], 1, 2)
     lt = local_transfer[0]
     up_rows = jnp.transpose(up_transfer, (1, 2, 0)).reshape(RANK * RANK, UPN)
-    n_remote = 96
+    n_remote = 112
 
     gathered, near, far, tp, scg, tcg = pl.pallas_call(
         gather_kernel,
@@ -636,9 +664,17 @@
             shape(PTS, PAIRS * 8, 128), shape(LEAFS, 8, 128, dtype=jnp.int32),
             shape(PTS, 8, 128, dtype=jnp.int32),
         ),
-        in_specs=[vmem()] * 5 + [anywhere()] + [vmem()] * 3,
+        in_specs=[anywhere()] * 7 + [vmem()] * 3,
         out_specs=(vmem(),) * 6,
         scratch_shapes=[
+            pltpu.VMEM((VEC, LEAVES * LEAF), F32),
+            pltpu.VMEM((3, LEAVES * LEAF), F32),
+            pltpu.VMEM((LEAVES, RANK, LEAF), F32),
+            pltpu.VMEM((30, RANK, RANK), F32),
+            pltpu.VMEM((3, PAIRS * 128), F32),
+            pltpu.VMEM((3, UPN * RANK), F32),
+            pltpu.VMEM((8, 128), jnp.int32),
+            pltpu.VMEM((8, 128), jnp.int32),
             pltpu.VMEM((18 * LEAF, DEPTH), BF16),
             pltpu.VMEM((DEPTH, 18 * LEAF), BF16),
             pltpu.VMEM((2 * VEC, 18 * LEAF), BF16),
@@ -647,18 +683,17 @@
             pltpu.VMEM((PAY_ROWS, 128), F32),
             pltpu.VMEM((PAIRS * 8, 128), F32),
             pltpu.VMEM((RANK * RANK, UPN), F32),
-            pltpu.VMEM((16 * RANK, RANK), F32),
-            pltpu.VMEM((UPPER, VEC, RANK), F32),
-            pltpu.VMEM((UPPER, VEC, RANK), F32),
+            pltpu.VMEM((48 * RANK, RANK), F32),
+            pltpu.VMEM((44, VEC, RANK), F32),
             pltpu.VMEM((UPPER, VEC, RANK), F32),
             pltpu.SemaphoreType.DMA((n_remote,)),
             pltpu.SemaphoreType.DMA((n_remote,)),
             pltpu.SemaphoreType.DMA((16,)),
         ],
         compiler_params=pltpu.CompilerParams(
-            collective_id=0, has_side_effects=True, vmem_limit_bytes=48 << 20
+            collective_id=0, has_side_effects=True, vmem_limit_bytes=63 << 20
         ),
-    )(vectors, points, leaf_bases, lt, skel_points, up_rows, up_points, source_code, target_code)
+    )(vectors, points, leaf_bases, lt, skel_points, up_rows, up_points, sources, targets, live_counts)
 
     partial = pl.pallas_call(
         couple_kernel,
@@ -681,7 +716,7 @@
             pltpu.VMEM(((NODES + 1) * RANK, 128), F32),
             pltpu.VMEM(((NODES + 1) * RANK, 128), F32),
         ],
-        compiler_params=pltpu.CompilerParams(vmem_limit_bytes=56 << 20),
+        compiler_params=pltpu.CompilerParams(vmem_limit_bytes=63 << 20),
     )(gathered, tp, scg, tcg)
 
     return pl.pallas_call(
@@ -704,7 +739,7 @@
             pltpu.SemaphoreType.DMA((8,)),
         ],
         compiler_params=pltpu.CompilerParams(
-            collective_id=1, has_side_effects=True, vmem_limit_bytes=48 << 20
+            collective_id=1, has_side_effects=True, vmem_limit_bytes=63 << 20
         ),
     )(partial, far, lt, leaf_bases, near)
 

time: 115 us -> 93.2 us (0.81)
  Pallas kernels: 101 us -> 91.1 us
  local copies, waits for them, and re-layouts: 11 us -> 1.87 us
  other arithmetic: 2.18 us -> 0 us
    unnamed x26 -> x1, local copies, waits for them, and re-layouts: 11 us -> 1.87 us
    pallas_call x1, Pallas kernels: 48.9 us -> 43 us  [on_device(): pl.pallas_call(gather_kernel, out_shape=(shape(LEAFS, PAY_ROWS, 128), sha...]
    pallas_call x1, Pallas kernels: 22.5 us -> 18.7 us  [on_device(): pl.pallas_call(scatter_kernel, out_shape=shape(VEC, LEAVES * LEAF), in_sp...]
where the time goes in v3:
time: 93.2 us; the launch traced here: 93 us
  Pallas kernels  91.1 us (98%)
  local copies, waits for them, and re-layouts  1.87 us (2%)
    pallas_call x1, Pallas kernels, on_device(): pl.pallas_call(gather_kernel, out_shape=(shape(LEAFS, PAY_ROWS, 128), sha...  43 us
    pallas_call x1, Pallas kernels, on_device(): pl.pallas_call(couple_kernel, out_shape=shape(PTS, COEF_ROWS, 128), in_sp...  29.3 us
    pallas_call x1, Pallas kernels, on_device(): pl.pallas_call(scatter_kernel, out_shape=shape(VEC, LEAVES * LEAF), in_sp...  18.7 us
    unnamed x1, local copies, waits for them, and re-layouts  1.87 us

profile of v3, /device:TPU:1, one launch (start us, length us, event | category | flops | bytes accessed | tf_op | source)
XLA Modules:
  0.0 93.0 jit_solution(10577085022337074157)
XLA Ops:
  0.0 43.0 %shard_map.100 = (f32[16,496,128]{2,1,0:T(8,128)}, f32[32,4096]{1,0:T(8,128)}, f32[32,64]{1,0:T(8,128)}, f32[8,112,128]{2,1,0:T(8,128)}, s32[16,8,128]{2,1,0:T(8,128)}, /*index=5*/s32[8,8,128]{2,1,0:T(8,128)}) custom-call(f32[32,4096]{1,0:T(8,128)} %vec_hbm.1, f32[3,4096]{1,0:T(4,128)} %pts_hbm.1, f32[16,64,256]{2,1,0:T(8,128)} %base_hbm.3, ...), custom_call_target="tpu_custom_call" | custom-call | tf_op jit(solution)/shard_map/pallas_call | solution.py:660
  43.0 29.3 %shard_map.101.acc_hbm = f32[8,448,128]{2,1,0:T(8,128)} custom-call(f32[16,496,128]{2,1,0:T(8,128)} %get-tuple-element.11.g_hbm, f32[8,112,128]{2,1,0:T(8,128)} %get-tuple-element.12.tp_hbm, s32[16,8,128]{2,1,0:T(8,128)} %get-tuple-element.13.sc_hbm, s32[8,8,128]{2,1,0:T(8,128)} %get-tuple-element.14.tc_hbm), custom_call_target="tpu_custom_call" | custom-call | tf_op jit(solution)/shard_map/pallas_call | solution.py:698
  72.4 18.7 %shard_map.102 = f32[32,4096]{1,0:T(8,128)} custom-call(f32[8,448,128]{2,1,0:T(8,128)} %shard_map.101.acc_hbm, f32[32,64]{1,0:T(8,128)} %get-tuple-element.15.far_hbm, f32[30,64,64]{2,1,0:T(8,128)} %bitcast.12, f32[16,64,256]{2,1,0:T(8,128)} %base_hbm.3, f32[32,4096]{1,0:T(8,128)} %get-tuple-element.16.near_hbm), custom_call_target="tpu_custom_call" | custom-call | tf_op jit(solution)/shard_map/pallas_call | solution.py:722
  91.1 1.9 %copy.12 = f32[32,4096]{1,0:T(8,128)} copy(f32[32,4096]{1,0:T(8,128)} %shard_map.102) | data formatting | bytes 1048576

commit v4 on v3

--- a/solution.py
+++ b/solution.py
@@ -236,6 +236,139 @@
     tree[p] = root
     roots = [remote(tree.at[p], tree.at[p], (leaf, p ^ k)) for k in range(1, PTS)]
 
+    local(pay, g_ref.at[leaf])
+
+    r48 = lax.broadcasted_iota(jnp.int32, (48, UPN), 0)
+    c48 = lax.broadcasted_iota(jnp.int32, (48, UPN), 1)
+    want = jnp.where(
+        r48 < 8, leaf * 8 + r48,
+        jnp.where(r48 < 12, 120 + leaf * 4 + r48, jnp.where(r48 < 14, 180 + leaf * 2 + r48, 210 + r48)),
+    )
+    pick = (c48 == want).astype(F32).astype(BF16)
+
+    def pick_rows(lo, hi):
+        @pl.loop(lo, hi)
+        def _(r):
+            halves = [
+                split(up_all[pl.ds(pl.multiple_of(r * 512 + i * 128, 128), 128), :])
+                for i in range(4)
+            ]
+            got = [dg(pick, h, NT) + dg(pick, l, NT) for h, l in halves]
+            for i, x in enumerate(got):
+                ut[pl.ds(8 * r + 2 * i, 48, stride=RANK), :] = x[:, :RANK]
+                ut[pl.ds(8 * r + 2 * i + 1, 48, stride=RANK), :] = x[:, RANK:]
+
+    opposite = {}
+
+    def step_a():
+        for h in range(2):
+            opposite[h] = forward(
+                h, 0, near_id(h, 0, -1), near_id(h, 0, 1), stage1[h, 1], stage1[h, -1]
+            )
+            spread(h, -1)
+            spread(h, 1)
+
+    def step_b():
+        for h in range(2):
+            opposite[h][0].wait_recv()
+            opposite[h][1].wait_recv()
+            spread(h, 2)
+
+    last = []
+
+    def step_c(first):
+        for h in range(2):
+            last.extend(
+                forward(
+                    h, 1, block_id(h, first, -1), block_id(h, first, 1),
+                    stage2[h, first, 1], stage2[h, first, -1],
+                )
+            )
+
+    def matrix(n):
+        return ut[pl.ds(pl.multiple_of(n * RANK, RANK), RANK), :]
+
+    def parent(n):
+        return dot3(
+            jnp.concatenate([tree[n], tree[n + 1]], axis=1),
+            jnp.concatenate([matrix(n), matrix(n + 1)], axis=1),
+            NT,
+        )
+
+    def raise_level(u):
+        return [parent(TREE[u] + 2 * i) for i in range((TREE[u + 1] - TREE[u]) // 2)]
+
+    def own_node(u):
+        return p >> u if u < 3 else leaf >> (u - 3)
+
+    def lower_levels():
+        for c in roots:
+            c.wait_recv()
+        for u in range(2):
+            for i, x in enumerate(raise_level(u)):
+                tree[TREE[u + 1] + i] = x
+        mine = TREE[3] + leaf
+        tree[mine] = raise_level(2)[0]
+        return [remote(tree.at[mine], tree.at[mine], (leaf ^ k, p)) for k in range(1, LEAFS)]
+
+    def upper_levels(tops):
+        for c in tops:
+            c.wait_recv()
+        for u in range(3, 6):
+            for i, x in enumerate(raise_level(u)):
+                tree[TREE[u + 1] + i] = x
+
+    def sibling_fields():
+        lane_left = lax.broadcasted_iota(jnp.int32, (VEC, 2 * RANK), 1) < RANK
+        distances = []
+        for u in range(UPPER):
+            first = lax.shift_right_logical(me, u + 1) * 2
+            col = pl.multiple_of((up_offset(u) + first) * RANK, 128)
+            u8, w8 = forms(scaled(upp_ref[:, pl.ds(col, 128)]))
+            distances.append(dg(stack_u(u8).T.astype(BF16), stack_w(w8).astype(BF16), NN))
+        kernels = [matern(x) for x in distances]
+        for u in range(UPPER):
+            left_side = lax.rem(own_node(u), 2) == 0
+            sib = tree[TREE[u] + (own_node(u) ^ 1)]
+            pair = jnp.concatenate([sib, sib], axis=1)
+            only_sib = jnp.where(jnp.logical_xor(lane_left, left_side), pair, 0.0)
+            out = dot3(only_sib, kernels[u], NN)
+            sf[u] = jnp.where(left_side, out[:, :RANK], out[:, RANK:])
+
+    def prepare(slot, vec, pts):
+        vh, vl = split(vec)
+        lanes = pl.ds(pl.multiple_of(slot * LEAF, LEAF), LEAF)
+        v_scr[0:VEC, lanes] = vh
+        v_scr[VEC:2 * VEC, lanes] = vl
+        u8, w8 = forms(scaled(pts))
+        w_scr[:, lanes] = stack_w(w8).astype(BF16)
+        u_scr[lanes, :] = stack_u(u8).T.astype(BF16)
+
+    def near(m):
+        lanes = pl.ds(pl.multiple_of(m * LEAF, LEAF), LEAF)
+        w = w_scr[:, lanes]
+        total = None
+        for b in range(3):
+            src = pl.ds(pl.multiple_of((m - 1 + b) * LEAF, LEAF), LEAF)
+            kh, kl = split(matern(dg(u_scr[src, :], w, NN)))
+            v = v_scr[:, src]
+            big = dg(v, kh, NN)
+            part = big[:VEC] + (big[VEC:] + dg(v[:VEC], kl, NN))
+            total = part if total is None else total + part
+        near_ref[:, pl.ds(pl.multiple_of((m - 1) * LEAF, LEAF), LEAF)] = total
+
+    def near_span(lo, hi):
+        @pl.loop(lo, hi)
+        def _(m):
+            near(m)
+
+    step_a()
+    locals_[6].wait()
+    pick_rows(0, 4)
+    step_b()
+    pick_rows(4, 8)
+    tops = lower_levels()
+    step_c(0)
     for i in (4, 5):
         locals_[i].wait()
     for side, off in ((0, 0), (1, (LEAVES - 1) * LEAF)):
@@ -255,139 +388,6 @@
     local(tc_ref, tcg_ref.at[p])
     local(sc_ref, scg_ref.at[leaf])
 
-    local(pay, g_ref.at[leaf])
-
-    r48 = lax.broadcasted_iota(jnp.int32, (48, UPN), 0)
-    c48 = lax.broadcasted_iota(jnp.int32, (48, UPN), 1)
-    want = jnp.where(
-        r48 < 8, leaf * 8 + r48,
-        jnp.where(r48 < 12, 120 + leaf * 4 + r48, jnp.where(r48 < 14, 180 + leaf * 2 + r48, 210 + r48)),
-    )
-    pick = (c48 == want).astype(F32).astype(BF16)
-
-    def pick_rows(lo, hi):
-        @pl.loop(lo, hi)
-        def _(r):
-            halves = [
-                split(up_all[pl.ds(pl.multiple_of(r * 512 + i * 128, 128), 128), :])
-                for i in range(4)
-            ]
-            got = [dg(pick, h, NT) + dg(pick, l, NT) for h, l in halves]
-            for i, x in enumerate(got):
-                ut[pl.ds(8 * r + 2 * i, 48, stride=RANK), :] = x[:, :RANK]
-                ut[pl.ds(8 * r + 2 * i + 1, 48, stride=RANK), :] = x[:, RANK:]
-
-    opposite = {}
-
-    def step_a():
-        for h in range(2):
-            opposite[h] = forward(
-                h, 0, near_id(h, 0, -1), near_id(h, 0, 1), stage1[h, 1], stage1[h, -1]
-            )
-            spread(h, -1)
-            spread(h, 1)
-
-    def step_b():
-        for h in range(2):
-            opposite[h][0].wait_recv()
-            opposite[h][1].wait_recv()
-            spread(h, 2)
-
-    last = []
-
-    def step_c(first):
-        for h in range(2):
-            last.extend(
-                forward(
-                    h, 1, block_id(h, first, -1), block_id(h, first, 1),
-                    stage2[h, first, 1], stage2[h, first, -1],
-                )
-            )
-
-    def matrix(n):
-        return ut[pl.ds(pl.multiple_of(n * RANK, RANK), RANK), :]
-
-    def parent(n):
-        return dot3(
-            jnp.concatenate([tree[n], tree[n + 1]], axis=1),
-            jnp.concatenate([matrix(n), matrix(n + 1)], axis=1),
-            NT,
-        )
-
-    def raise_level(u):
-        return [parent(TREE[u] + 2 * i) for i in range((TREE[u + 1] - TREE[u]) // 2)]
-
-    def own_node(u):
-        return p >> u if u < 3 else leaf >> (u - 3)
-
-    def lower_levels():
-        for c in roots:
-            c.wait_recv()
-        for u in range(2):
-            for i, x in enumerate(raise_level(u)):
-                tree[TREE[u + 1] + i] = x
-        mine = TREE[3] + leaf
-        tree[mine] = raise_level(2)[0]
-        return [remote(tree.at[mine], tree.at[mine], (leaf ^ k, p)) for k in range(1, LEAFS)]
-
-    def upper_levels(tops):
-        for c in tops:
-            c.wait_recv()
-        for u in range(3, 6):
-            for i, x in enumerate(raise_level(u)):
-                tree[TREE[u + 1] + i] = x
-
-    def sibling_fields():
-        lane_left = lax.broadcasted_iota(jnp.int32, (VEC, 2 * RANK), 1) < RANK
-        distances = []
-        for u in range(UPPER):
-            first = lax.shift_right_logical(me, u + 1) * 2
-            col = pl.multiple_of((up_offset(u) + first) * RANK, 128)
-            u8, w8 = forms(scaled(upp_ref[:, pl.ds(col, 128)]))
-            distances.append(dg(stack_u(u8).T.astype(BF16), stack_w(w8).astype(BF16), NN))
-        kernels = [matern(x) for x in distances]
-        for u in range(UPPER):
-            left_side = lax.rem(own_node(u), 2) == 0
-            sib = tree[TREE[u] + (own_node(u) ^ 1)]
-            pair = jnp.concatenate([sib, sib], axis=1)
-            only_sib = jnp.where(jnp.logical_xor(lane_left, left_side), pair, 0.0)
-            out = dot3(only_sib, kernels[u], NN)
-            sf[u] = jnp.where(left_side, out[:, :RANK], out[:, RANK:])
-
-    def prepare(slot, vec, pts):
-        vh, vl = split(vec)
-        lanes = pl.ds(pl.multiple_of(slot * LEAF, LEAF), LEAF)
-        v_scr[0:VEC, lanes] = vh
-        v_scr[VEC:2 * VEC, lanes] = vl
-        u8, w8 = forms(scaled(pts))
-        w_scr[:, lanes] = stack_w(w8).astype(BF16)
-        u_scr[lanes, :] = stack_u(u8).T.astype(BF16)
-
-    def near(m):
-        lanes = pl.ds(pl.multiple_of(m * LEAF, LEAF), LEAF)
-        w = w_scr[:, lanes]
-        total = None
-        for b in range(3):
-            src = pl.ds(pl.multiple_of((m - 1 + b) * LEAF, LEAF), LEAF)
-            kh, kl = split(matern(dg(u_scr[src, :], w, NN)))
-            v = v_scr[:, src]
-            big = dg(v, kh, NN)
-            part = big[:VEC] + (big[VEC:] + dg(v[:VEC], kl, NN))
-            total = part if total is None else total + part
-        near_ref[:, pl.ds(pl.multiple_of((m - 1) * LEAF, LEAF), LEAF)] = total
-
-    def near_span(lo, hi):
-        @pl.loop(lo, hi)
-        def _(m):
-            near(m)
-
-    step_a()
-    locals_[6].wait()
-    pick_rows(0, 4)
-    step_b()
-    pick_rows(4, 8)
-    tops = lower_levels()
-    step_c(0)
 
     @pl.loop(0, LEAVES)
     def _(m):
@@ -399,8 +399,8 @@
     near_span(6, 10)
     step_c(1)
     near_span(10, 12)
+    step_c(2)
     upper_levels(tops)
-    step_c(2)
     near_span(12, 16)
     sibling_fields()
     h0.wait_recv()
@@ -427,7 +427,7 @@
 
 
 def couple_kernel(
-    g_hbm, tp_hbm, sc_hbm, tc_hbm, o_ref, g_ref, tp_ref, sc_ref, tc_ref, sem, ct, wt, ut, masks, sums, d_scr, k_scr, acc_a, acc_b,
+    g_hbm, tp_hbm, sc_hbm, tc_hbm, o_ref, g_ref, tp_ref, sc_ref, tc_ref, sem, ct, wt, ut, masks, sums, d_scr, k_scr, acc_a, acc_b, used,
 ):
     leaf = lax.axis_index("leaf")
     p = lax.axis_index("pts")
@@ -458,9 +458,17 @@
     def masked(x, m):
         return (x.reshape(-1, 16, 128) * masks[m][None]).reshape(x.shape)
 
-    @pl.loop(0, LEAFS)
-    def _(s):
+    for copy in others:
+        copy.wait()
+
+    def fill(s, count):
         pltpu.make_async_copy(g_hbm.at[s], g_ref.at[s], sem.at[s]).wait()
+        for d in range(PTS):
+            for row in range(6):
+                r = tc_ref[d, row, s * PTS + p]
+                n = s * NODES + sc_ref[s, row, leaf * PTS + d]
+                used[count] = n * 256 + (r + d * (NODES + 1))
+                count = count + (r < NODES).astype(jnp.int32)
         for g in range(GROUPS):
             c = g_ref[s, g * RANK:(g + 1) * RANK, :]
             for j in range(2):
@@ -482,50 +490,58 @@
                     pltpu.roll(w, RANK, 1) if j else w
                 ).astype(BF16)
 
-    for copy in others:
-        copy.wait()
-    ut[NODES * RANK:(NODES + 1) * RANK, :] = jnp.zeros((RANK, 2 * DEPTH), BF16)
+        return count
+
+    total = lax.fori_loop(0, LEAFS, fill, jnp.int32(0))
+    for i in range(2 * LEAFS):
+        used[total + i] = NODES
     slot_a = lax.broadcasted_iota(jnp.int32, (RANK, 2 * DEPTH), 1) < DEPTH
 
     @pl.loop(0, PTS)
     def _(d):
+        first = d * (NODES + 1)
         for a in range(PAIRS):
             t = stack_u(tp_ref[d, a * 8:(a + 1) * 8, :])
-            ut[2 * a * RANK:(2 * a + 2) * RANK, :] = jnp.concatenate([t, t], axis=0).T.astype(BF16)
-        acc_a[...] = jnp.zeros_like(acc_a)
-        acc_b[...] = jnp.zeros_like(acc_b)
-
-        @pl.loop(0, 3)
-        def _(lev):
-            ids = []
-            for s in range(LEAFS):
-                na = s * NODES + sc_ref[s, lev * 2, leaf * PTS + d]
-                nb = s * NODES + sc_ref[s, lev * 2 + 1, leaf * PTS + d]
-                ra = rows_of(tc_ref[d, lev * 2, s * PTS + p], RANK)
-                rb = rows_of(tc_ref[d, lev * 2 + 1, s * PTS + p], RANK)
-                ids.append((na, nb, ra, rb))
-            for s, (na, nb, ra, rb) in enumerate(ids):
-                u = jnp.where(slot_a, ut[ra, :], ut[rb, :])
-                wa = masked(wt[rows_of(na, DEPTH), :], 4)
-                wb = masked(wt[rows_of(nb ^ 1, DEPTH), :], 5)
-                d_scr[s * RANK:(s + 1) * RANK] = dg(u, jnp.concatenate([wa, wb], axis=0), NN)
-            for s in range(LEAFS):
-                h, l = split(matern(d_scr[s * RANK:(s + 1) * RANK]))
-                k_scr[s * RANK:(s + 1) * RANK] = jnp.concatenate([h, l, h], axis=1)
-            for s, (na, nb, ra, rb) in enumerate(ids):
-                xa = masked(ct[rows_of(na >> 1, 2 * RANK), :], na & 1)
-                xb = masked(ct[rows_of((nb >> 1) ^ 1, 2 * RANK), :], 2 + (nb & 1))
-                high = jnp.concatenate([xa[:RANK], xb[:RANK]], axis=0)
-                rest = jnp.concatenate([xa[RANK:], xb[RANK:]], axis=0)
-                k = k_scr[s * RANK:(s + 1) * RANK]
-                part = dg(k, jnp.concatenate([high, high, rest], axis=0), NN)
-                acc_a[ra, :] += part
-                acc_b[rb, :] += part
-
+            rows = pl.ds(pl.multiple_of((first + 2 * a) * RANK, RANK), 2 * RANK)
+            ut[rows, :] = jnp.concatenate([t, t], axis=0).T.astype(BF16)
+        ut[rows_of(first + NODES, RANK), :] = jnp.zeros((RANK, 2 * DEPTH), BF16)
+        rows = pl.ds(pl.multiple_of(first * RANK, RANK), (NODES + 1) * RANK)
+        acc_a[rows, :] = jnp.zeros(((NODES + 1) * RANK, 128), F32)
+        acc_b[rows, :] = jnp.zeros(((NODES + 1) * RANK, 128), F32)
+
+    def step(g, carry):
+        ids = []
+        for t in range(LEAFS):
+            a = used[g * 2 * LEAFS + 2 * t]
+            b = used[g * 2 * LEAFS + 2 * t + 1]
+            ids.append((a >> 8, b >> 8, rows_of(a & 255, RANK), rows_of(b & 255, RANK)))
+        for s, (na, nb, ra, rb) in enumerate(ids):
+            u = jnp.where(slot_a, ut[ra, :], ut[rb, :])
+            wa = masked(wt[rows_of(na, DEPTH), :], 4)
+            wb = masked(wt[rows_of(nb ^ 1, DEPTH), :], 5)
+            d_scr[s * RANK:(s + 1) * RANK] = dg(u, jnp.concatenate([wa, wb], axis=0), NN)
+        for s in range(LEAFS):
+            h, l = split(matern(d_scr[s * RANK:(s + 1) * RANK]))
+            k_scr[s * RANK:(s + 1) * RANK] = jnp.concatenate([h, l, h], axis=1)
+        for s, (na, nb, ra, rb) in enumerate(ids):
+            xa = masked(ct[rows_of(na >> 1, 2 * RANK), :], na & 1)
+            xb = masked(ct[rows_of((nb >> 1) ^ 1, 2 * RANK), :], 2 + (nb & 1))
+            high = jnp.concatenate([xa[:RANK], xb[:RANK]], axis=0)
+            rest = jnp.concatenate([xa[RANK:], xb[RANK:]], axis=0)
+            k = k_scr[s * RANK:(s + 1) * RANK]
+            part = dg(k, jnp.concatenate([high, high, rest], axis=0), NN)
+            acc_a[ra, :] += part
+            acc_b[rb, :] += part
+        return carry
+
+    lax.fori_loop(0, (total + 2 * LEAFS - 1) >> 5, step, 0)
+
+    @pl.loop(0, PTS)
+    def _(d):
         for g in range(GROUPS):
             parts = []
             for q in range(4):
-                rows = slice((4 * g + q) * RANK, (4 * g + q + 1) * RANK)
+                rows = rows_of(d * (NODES + 1) + 4 * g + q, RANK)
                 parts.append(jnp.where(low, acc_a[rows, :], acc_b[rows, :]))
             h, l = split(jnp.concatenate(parts, axis=1))
             o_ref[d, g * RANK:(g + 1) * RANK, :] = dg(h, sums[...], NN) + dg(l, sums[...], NN)
@@ -708,13 +724,14 @@
             pltpu.SemaphoreType.DMA((LEAFS + 3,)),
             pltpu.VMEM((LEAFS * GROUPS * 4 * RANK, 128), BF16),
             pltpu.VMEM((LEAFS * NODES * DEPTH, 128), BF16),
-            pltpu.VMEM(((NODES + 1) * RANK, 2 * DEPTH), BF16),
+            pltpu.VMEM((PTS * (NODES + 1) * RANK, 2 * DEPTH), BF16),
             pltpu.VMEM((8, 16, 128), BF16),
             pltpu.VMEM((512, 128), BF16),
             pltpu.VMEM((LEAFS * RANK, 128), F32),
             pltpu.VMEM((LEAFS * RANK, 3 * 128), BF16),
-            pltpu.VMEM(((NODES + 1) * RANK, 128), F32),
-            pltpu.VMEM(((NODES + 1) * RANK, 128), F32),
+            pltpu.VMEM((PTS * (NODES + 1) * RANK, 128), F32),
+            pltpu.VMEM((PTS * (NODES + 1) * RANK, 128), F32),
+            pltpu.SMEM((1024,), jnp.int32),
         ],
         compiler_params=pltpu.CompilerParams(vmem_limit_bytes=63 << 20),
     )(gathered, tp, scg, tcg)

time: 93.2 us -> 87.8 us (0.942)
  Pallas kernels: 91.1 us -> 86 us
    pallas_call x1, Pallas kernels: 29.3 us -> 24.9 us  [on_device(): pl.pallas_call(couple_kernel, out_shape=shape(PTS, COEF_ROWS, 128), in_sp...]
    pallas_call x1, Pallas kernels: 43 us -> 42.1 us  [on_device(): pl.pallas_call(gather_kernel, out_shape=(shape(LEAFS, PAY_ROWS, 128), sha...]
where the time goes in v4:
time: 87.8 us; the launch traced here: 87.9 us
  Pallas kernels  86 us (98%)
  local copies, waits for them, and re-layouts  1.87 us (2%)
    pallas_call x1, Pallas kernels, on_device(): pl.pallas_call(gather_kernel, out_shape=(shape(LEAFS, PAY_ROWS, 128), sha...  42.1 us
    pallas_call x1, Pallas kernels, on_device(): pl.pallas_call(couple_kernel, out_shape=shape(PTS, COEF_ROWS, 128), in_sp...  24.9 us
    pallas_call x1, Pallas kernels, on_device(): pl.pallas_call(scatter_kernel, out_shape=shape(VEC, LEAVES * LEAF), in_sp...  19 us
    unnamed x1, local copies, waits for them, and re-layouts  1.87 us

profile of v4, /device:TPU:1, one launch (start us, length us, event | category | flops | bytes accessed | tf_op | source)
XLA Modules:
  0.0 87.9 jit_solution(14478261641294088777)
XLA Ops:
  0.0 42.1 %shard_map.100 = (f32[16,496,128]{2,1,0:T(8,128)}, f32[32,4096]{1,0:T(8,128)}, f32[32,64]{1,0:T(8,128)}, f32[8,112,128]{2,1,0:T(8,128)}, s32[16,8,128]{2,1,0:T(8,128)}, /*index=5*/s32[8,8,128]{2,1,0:T(8,128)}) custom-call(f32[32,4096]{1,0:T(8,128)} %vec_hbm.1, f32[3,4096]{1,0:T(4,128)} %pts_hbm.1, f32[16,64,256]{2,1,0:T(8,128)} %base_hbm.3, ...), custom_call_target="tpu_custom_call" | custom-call | tf_op jit(solution)/shard_map/pallas_call | solution.py:676
  42.1 24.9 %shard_map.101.acc_hbm = f32[8,448,128]{2,1,0:T(8,128)} custom-call(f32[16,496,128]{2,1,0:T(8,128)} %get-tuple-element.11.g_hbm, f32[8,112,128]{2,1,0:T(8,128)} %get-tuple-element.12.tp_hbm, s32[16,8,128]{2,1,0:T(8,128)} %get-tuple-element.13.sc_hbm, s32[8,8,128]{2,1,0:T(8,128)} %get-tuple-element.14.tc_hbm), custom_call_target="tpu_custom_call" | custom-call | tf_op jit(solution)/shard_map/pallas_call | solution.py:714
  67.0 19.0 %shard_map.102 = f32[32,4096]{1,0:T(8,128)} custom-call(f32[8,448,128]{2,1,0:T(8,128)} %shard_map.101.acc_hbm, f32[32,64]{1,0:T(8,128)} %get-tuple-element.15.far_hbm, f32[30,64,64]{2,1,0:T(8,128)} %bitcast.12, f32[16,64,256]{2,1,0:T(8,128)} %base_hbm.3, f32[32,4096]{1,0:T(8,128)} %get-tuple-element.16.near_hbm), custom_call_target="tpu_custom_call" | custom-call | tf_op jit(solution)/shard_map/pallas_call | solution.py:739
  86.0 1.9 %copy.12 = f32[32,4096]{1,0:T(8,128)} copy(f32[32,4096]{1,0:T(8,128)} %shard_map.102) | data formatting | bytes 1048576

commit v5 on v4

--- a/solution.py
+++ b/solution.py
@@ -29,6 +29,7 @@
 UPN = 254
 TREE = (0, 8, 12, 14, 30, 38, 42, 44)
 GROUPS = NODES // 4
+BATCH = 32
 DEPTH = 48
 NN = (((1,), (0,)), ((), ()))
 NT = (((1,), (1,)), ((), ()))
@@ -151,8 +152,9 @@
         shift = LEAVES * 2 - (LEAVES * 2 >> lev) - me * (LEAVES >> lev)
         for k in range(2):
             row = slice(2 * lev + k, 2 * lev + k + 1)
-            sc_ref[row] = src_ref[lev, k:k + 1] + shift
-            tc_ref[row] = jnp.where(k < live_ref[lev], tgt_ref[lev, k:k + 1] + shift, NODES)
+            sc_ref[row] = (src_ref[lev, k:k + 1] + (shift + leaf * NODES)) * 256
+            target = jnp.where(k < live_ref[lev], tgt_ref[lev, k:k + 1] + shift, NODES)
+            tc_ref[row] = target + p * (NODES + 1)
 
     locals_[0].wait()
     pay[PAY_ROWS - 8:PAY_ROWS] = jnp.zeros((8, 128), F32)
@@ -466,9 +468,8 @@
         for d in range(PTS):
             for row in range(6):
                 r = tc_ref[d, row, s * PTS + p]
-                n = s * NODES + sc_ref[s, row, leaf * PTS + d]
-                used[count] = n * 256 + (r + d * (NODES + 1))
-                count = count + (r < NODES).astype(jnp.int32)
+                used[count] = sc_ref[s, row, leaf * PTS + d] + r
+                count = count + (r < d * (NODES + 1) + NODES).astype(jnp.int32)
         for g in range(GROUPS):
             c = g_ref[s, g * RANK:(g + 1) * RANK, :]
             for j in range(2):
@@ -492,9 +493,12 @@
 
         return count
 
-    total = lax.fori_loop(0, LEAFS, fill, jnp.int32(0))
-    for i in range(2 * LEAFS):
-        used[total + i] = NODES
+    for i in range(BATCH):
+        used[i] = NODES
+    end = lax.fori_loop(0, LEAFS, fill, jnp.int32(BATCH))
+    for i in range(2 * BATCH):
+        used[end + i] = NODES
+    k_scr[...] = jnp.zeros_like(k_scr)
     slot_a = lax.broadcasted_iota(jnp.int32, (RANK, 2 * DEPTH), 1) < DEPTH
 
     @pl.loop(0, PTS)
@@ -510,31 +514,34 @@
         acc_b[rows, :] = jnp.zeros(((NODES + 1) * RANK, 128), F32)
 
     def step(g, carry):
-        ids = []
+        def entry(i):
+            e = used[g * BATCH + i]
+            return e >> 8, rows_of(e & 255, RANK)
+
         for t in range(LEAFS):
-            a = used[g * 2 * LEAFS + 2 * t]
-            b = used[g * 2 * LEAFS + 2 * t + 1]
-            ids.append((a >> 8, b >> 8, rows_of(a & 255, RANK), rows_of(b & 255, RANK)))
-        for s, (na, nb, ra, rb) in enumerate(ids):
+            na, ra = entry(BATCH + 2 * t)
+            nb, rb = entry(BATCH + 2 * t + 1)
             u = jnp.where(slot_a, ut[ra, :], ut[rb, :])
             wa = masked(wt[rows_of(na, DEPTH), :], 4)
             wb = masked(wt[rows_of(nb ^ 1, DEPTH), :], 5)
-            d_scr[s * RANK:(s + 1) * RANK] = dg(u, jnp.concatenate([wa, wb], axis=0), NN)
-        for s in range(LEAFS):
-            h, l = split(matern(d_scr[s * RANK:(s + 1) * RANK]))
-            k_scr[s * RANK:(s + 1) * RANK] = jnp.concatenate([h, l, h], axis=1)
-        for s, (na, nb, ra, rb) in enumerate(ids):
+            d_scr[t * RANK:(t + 1) * RANK] = dg(u, jnp.concatenate([wa, wb], axis=0), NN)
+        for t in range(LEAFS):
+            na, ra = entry(2 * t)
+            nb, rb = entry(2 * t + 1)
             xa = masked(ct[rows_of(na >> 1, 2 * RANK), :], na & 1)
             xb = masked(ct[rows_of((nb >> 1) ^ 1, 2 * RANK), :], 2 + (nb & 1))
             high = jnp.concatenate([xa[:RANK], xb[:RANK]], axis=0)
             rest = jnp.concatenate([xa[RANK:], xb[RANK:]], axis=0)
-            k = k_scr[s * RANK:(s + 1) * RANK]
-            part = dg(k, jnp.concatenate([high, high, rest], axis=0), NN)
+            part = dg(
+                k_scr[t * RANK:(t + 1) * RANK], jnp.concatenate([high, high, rest], axis=0), NN
+            )
             acc_a[ra, :] += part
             acc_b[rb, :] += part
+            h, l = split(matern(d_scr[t * RANK:(t + 1) * RANK]))
+            k_scr[t * RANK:(t + 1) * RANK] = jnp.concatenate([h, l, h], axis=1)
         return carry
 
-    lax.fori_loop(0, (total + 2 * LEAFS - 1) >> 5, step, 0)
+    lax.fori_loop(0, (end + BATCH - 1) // BATCH, step, 0)
 
     @pl.loop(0, PTS)
     def _(d):

time: 87.8 us -> 87.8 us (level)
  no operation moved by 1% of the time
where the time goes in v5:
time: 87.8 us; the launch traced here: 87.5 us
  Pallas kernels  85.6 us (97%)
  local copies, waits for them, and re-layouts  1.87 us (2%)
    pallas_call x1, Pallas kernels, on_device(): pl.pallas_call(gather_kernel, out_shape=(shape(LEAFS, PAY_ROWS, 128), sha...  42.1 us
    pallas_call x1, Pallas kernels, on_device(): pl.pallas_call(couple_kernel, out_shape=shape(PTS, COEF_ROWS, 128), in_sp...  24.2 us
    pallas_call x1, Pallas kernels, on_device(): pl.pallas_call(scatter_kernel, out_shape=shape(VEC, LEAVES * LEAF), in_sp...  19.3 us
    unnamed x1, local copies, waits for them, and re-layouts  1.87 us

profile of v5, /device:TPU:1, one launch (start us, length us, event | category | flops | bytes accessed | tf_op | source)
XLA Modules:
  0.0 87.5 jit_solution(2088186755130947521)
XLA Ops:
  0.0 42.1 %shard_map.100 = (f32[16,496,128]{2,1,0:T(8,128)}, f32[32,4096]{1,0:T(8,128)}, f32[32,64]{1,0:T(8,128)}, f32[8,112,128]{2,1,0:T(8,128)}, s32[16,8,128]{2,1,0:T(8,128)}, /*index=5*/s32[8,8,128]{2,1,0:T(8,128)}) custom-call(f32[32,4096]{1,0:T(8,128)} %vec_hbm.1, f32[3,4096]{1,0:T(4,128)} %pts_hbm.1, f32[16,64,256]{2,1,0:T(8,128)} %base_hbm.3, ...), custom_call_target="tpu_custom_call" | custom-call | tf_op jit(solution)/shard_map/pallas_call | solution.py:683
  42.1 24.2 %shard_map.101.acc_hbm = f32[8,448,128]{2,1,0:T(8,128)} custom-call(f32[16,496,128]{2,1,0:T(8,128)} %get-tuple-element.11.g_hbm, f32[8,112,128]{2,1,0:T(8,128)} %get-tuple-element.12.tp_hbm, s32[16,8,128]{2,1,0:T(8,128)} %get-tuple-element.13.sc_hbm, s32[8,8,128]{2,1,0:T(8,128)} %get-tuple-element.14.tc_hbm), custom_call_target="tpu_custom_call" | custom-call | tf_op jit(solution)/shard_map/pallas_call | solution.py:721
  66.4 19.3 %shard_map.102 = f32[32,4096]{1,0:T(8,128)} custom-call(f32[8,448,128]{2,1,0:T(8,128)} %shard_map.101.acc_hbm, f32[32,64]{1,0:T(8,128)} %get-tuple-element.15.far_hbm, f32[30,64,64]{2,1,0:T(8,128)} %bitcast.12, f32[16,64,256]{2,1,0:T(8,128)} %base_hbm.3, f32[32,4096]{1,0:T(8,128)} %get-tuple-element.16.near_hbm), custom_call_target="tpu_custom_call" | custom-call | tf_op jit(solution)/shard_map/pallas_call | solution.py:746
  85.7 1.9 %copy.12 = f32[32,4096]{1,0:T(8,128)} copy(f32[32,4096]{1,0:T(8,128)} %shard_map.102) | data formatting | bytes 1048576
